TPU v7x, 256 devices: a whole 4x4x8 slice. The times are simulated.
256 devices in a mesh: grp: 8 (over z_hi, core), fsdp: 32 (over y, x, z_lo).
Axes of the slice: x: 4, y: 4, z: 8 (z_hi: 4, z_lo: 2; z = z_hi * 2 + z_lo), core: 2. Of those that a mesh axis runs over, the one named last changes fastest.
Arguments:
- queries: bfloat16 [32, 1024, 4096], P('fsdp', 'grp')
- out_grad: bfloat16 [32, 1024, 4096], P('fsdp', 'grp'), may hold values from -6 to 6
- resp_in: bfloat16 [32, 1024, 5120], P('fsdp', 'grp'), may hold values from -6 to 6
- prompt_in: bfloat16 [32, 512, 5120], P('fsdp', 'grp'), may hold values from -6 to 6
- key_matrix: bfloat16 [5120, 512], P('fsdp'), may hold values from -0.078125 to 0.078125
- value_matrix: bfloat16 [5120, 512], P('fsdp'), may hold values from -0.078125 to 0.078125
- key_gain: float32 [128], replicated, may hold values from 0.1 to 1.9
- seg_prompt: int32 [32, 16], P('fsdp', 'grp'), may hold values from 0 to 7, as said below
- seg_start: int32 [32, 16], P('fsdp', 'grp'), may hold values from 0 to 112, as said below
- seg_len: int32 [32, 16], P('fsdp', 'grp'), may hold values from 1 to 112, as said below
- owner: int32 [32, 8], P('fsdp'), may hold values from 0 to 7, as said below
Outputs:
- query_grad: bfloat16 [32, 1024, 4096], P('fsdp', 'grp')
- resp_grad: bfloat16 [32, 1024, 5120], P('fsdp', 'grp')
- prompt_grad: bfloat16 [32, 512, 5120], P('fsdp', 'grp')
- key_weight_grad: bfloat16 [5120, 512], P('fsdp')
- value_weight_grad: bfloat16 [5120, 512], P('fsdp')
Inputs may be any that keep to these rules, and one draw needn't show every extreme that they name: `owner`: each row of the grp devices of one group is a permutation of 0 to 7. `seg_prompt`: within one group every prompt is named exactly 2 times. `seg_start`: on each device the starts rise, the first is 0, all are multiples of 16, and each response ends no later than the next one starts (the last one within the device's slots). `seg_len`: each response ends within the 16 slots before the next start (or the device's end).
All inputs are finite; a program needn't handle non-finite values.
Results may differ from a plain program's by a relative error of at most 0.04.
The roundings to bfloat16 on the way count: a program that leaves them out, or rounds other values in their place, can miss the bound.
Values may be sent and summed in bfloat16 or wider, within the bound.
A program may use at most 128 MiB of HBM per device.

v0:
```python
import functools
import math

import jax
import jax.numpy as jnp
import numpy as np
from jax import lax
from jax.experimental import pallas as pl
from jax.experimental.pallas import tpu as pltpu
from jax.sharding import PartitionSpec as P

MESH = pl.DeviceIdType.MESH
HBM = pl.BlockSpec(memory_space=pltpu.HBM)
SMEM = pl.BlockSpec(memory_space=pltpu.SMEM)
VMEM = pl.BlockSpec(memory_space=pltpu.VMEM)
VMEM_LIMIT = 60 * 1024 * 1024

WIDTH = 5120
HEAD = 128
ROWS = 160
HALF = 80
TOK = 128
PRO = 64
DEV = TOK + PRO
SCALE = 1.0 / math.sqrt(HEAD)
BASE = 1000000.0
bf16 = jnp.bfloat16
f32 = jnp.float32


def rotary_tables():
    frequency = np.float32(BASE) ** (-np.arange(64, dtype=np.float32) / np.float32(64))
    angles = np.arange(-128, 192, dtype=np.float32)[:, None] * frequency[None, :].astype(np.float32)
    angles = angles.astype(np.float32).astype(np.float64)
    cos, sin = np.cos(angles), np.sin(angles)
    return (
        np.concatenate([cos, cos], 1).astype(np.float32),
        np.concatenate([-sin, sin], 1).astype(np.float32),
    )


class Place:
    def __init__(self):
        g, f = lax.axis_index("grp"), lax.axis_index("fsdp")
        self.core, self.zh = lax.rem(g, 2), lax.div(g, 2)
        self.zl = lax.rem(f, 2)
        self.x = lax.rem(lax.div(f, 2), 4)
        self.y = lax.div(f, 8)
        self.z = self.zh * 2 + self.zl

    def at(self, y=None, x=None, z=None, core=None):
        y = self.y if y is None else y
        x = self.x if x is None else x
        z = self.z if z is None else z
        core = self.core if core is None else core
        return {"grp": lax.div(z, 2) * 2 + core, "fsdp": (y * 4 + x) * 2 + lax.rem(z, 2)}

    def ring_x(self):
        return self.x, self.at(x=lax.rem(self.x + 3, 4)), self.at(x=lax.rem(self.x + 1, 4))

    def ring_y(self):
        return self.y, self.at(y=lax.rem(self.y + 3, 4)), self.at(y=lax.rem(self.y + 1, 4))

    def ring_zh(self):
        return self.zh, self.at(z=lax.rem(self.z + 6, 8)), self.at(z=lax.rem(self.z + 2, 8))

    def near_z(self):
        return self.at(z=lax.rem(self.z + 7, 8)), self.at(z=lax.rem(self.z + 1, 8))

    def partner(self):
        return self.at(core=1 - self.core)


def greet(devices):
    barrier = pltpu.get_barrier_semaphore()
    for device in devices:
        pl.semaphore_signal(barrier, inc=1, device_id=device, device_id_type=MESH)
    pl.semaphore_wait(barrier, len(devices))


class Links:
    def __init__(self, send, recv):
        self.send, self.recv, self.used, self.sent = send, recv, 0, []

    def take(self):
        self.used += 1
        return self.used - 1

    def copy(self, number, src, dst, device):
        return pltpu.make_async_remote_copy(
            src_ref=src,
            dst_ref=dst,
            send_sem=self.send.at[number],
            recv_sem=self.recv.at[number],
            device_id=device,
            device_id_type=MESH,
        )

    def start(self, number, src, dst, device):
        made = self.copy(number, src, dst, device)
        made.start()
        self.sent.append(made)

    def arrived(self, number, dst, device):
        self.copy(number, dst, dst, device).wait_recv()

    def drain(self):
        for made in self.sent:
            made.wait_send()
        self.sent = []


class Gather4:
    def __init__(self, links, ring, view, half, own=None):
        self.links, self.view, self.half = links, view, half
        self.me, self.minus, self.plus = ring
        self.own = view(self.me) if own is None else own
        self.n = [links.take() for _ in range(4)]

    def begin(self):
        self.links.start(self.n[0], self.own, self.view(self.me), self.plus)
        self.links.start(self.n[1], self.own, self.view(self.me), self.minus)

    def forward(self):
        left, right = lax.rem(self.me + 3, 4), lax.rem(self.me + 1, 4)
        self.links.arrived(self.n[0], self.view(left), self.plus)
        self.links.start(self.n[2], self.half(left, 0), self.half(left, 0), self.plus)
        self.links.arrived(self.n[1], self.view(right), self.minus)
        self.links.start(self.n[3], self.half(right, 1), self.half(right, 1), self.minus)

    def finish(self):
        across = lax.rem(self.me + 2, 4)
        self.links.arrived(self.n[2], self.half(across, 0), self.plus)
        self.links.arrived(self.n[3], self.half(across, 1), self.minus)


class Reduce4:
    def __init__(self, links, ring, part, slot, add):
        self.links, self.part, self.slot, self.add = links, part, slot, add
        self.me, self.minus, self.plus = ring
        self.n = [links.take() for _ in range(6)]

    def send_for(self, place):
        part, slot, n = self.part, self.slot, self.n
        block = lax.rem(self.me + place, 4)
        if place == 2:
            self.links.start(n[0], part(block, 0), slot(0), self.plus)
            self.links.start(n[1], part(block, 1), slot(1), self.minus)
        if place == 1:
            self.links.start(n[2], part(block, 1), slot(2), self.plus)
        if place == 3:
            self.links.start(n[3], part(block, 0), slot(3), self.minus)

    def begin(self):
        for place in (2, 1, 3):
            self.send_for(place)

    def mid(self):
        left, right = lax.rem(self.me + 3, 4), lax.rem(self.me + 1, 4)
        part, slot, n = self.part, self.slot, self.n
        self.links.arrived(n[0], slot(0), self.plus)
        self.add(slot(0), [slot(0), part(right, 0)])
        self.links.start(n[4], slot(0), slot(4), self.plus)
        self.links.arrived(n[1], slot(1), self.minus)
        self.add(slot(1), [slot(1), part(left, 1)])
        self.links.start(n[5], slot(1), slot(5), self.minus)

    def finish(self, out):
        part, slot, n = self.part, self.slot, self.n
        self.links.arrived(n[3], slot(3), self.minus)
        self.links.arrived(n[4], slot(4), self.plus)
        self.add(out(0), [part(self.me, 0), slot(3), slot(4)])
        self.links.arrived(n[2], slot(2), self.plus)
        self.links.arrived(n[5], slot(5), self.minus)
        self.add(out(1), [part(self.me, 1), slot(2), slot(5)])


def add_block(dst, terms):
    total = terms[0][...].astype(f32)
    for term in terms[1:]:
        total = total + term[...].astype(f32)
    dst[...] = total.astype(dst.dtype)


def add_blocks(dst, terms):
    def body(i, carry):
        total = terms[0][i].astype(f32)
        for term in terms[1:]:
            total = total + term[i].astype(f32)
        dst[i] = total.astype(dst.dtype)
        return carry

    lax.fori_loop(0, dst.shape[0], body, 0)


def remote_params(number):
    return pltpu.CompilerParams(
        collective_id=number, has_side_effects=True, vmem_limit_bytes=VMEM_LIMIT
    )


LOCAL = pltpu.CompilerParams(vmem_limit_bytes=VMEM_LIMIT)


GATHER_COPIES = 64


def gather_kernel(kw, vw, resp, prompt, q, og, sp, ss, sl, W, XP, QP, OP, SP, SS, SL, send, recv, local):
    me = Place()
    core, partner = me.core, me.partner()
    near_minus, near_plus = me.near_z()
    _, xm, xp = me.ring_x()
    _, ym, yp = me.ring_y()
    greet([xm, xp, ym, yp, near_minus, near_plus, partner])
    links = Links(send, recv)

    def columns(matrix, j):
        return matrix.at[:, pl.ds(pl.multiple_of((core * 2 + j) * HEAD, HEAD), HEAD)]

    own = [columns(kw, 0), columns(kw, 1), columns(vw, 0), columns(vw, 1)]
    x, y, zl = me.x, me.y, me.zl
    rows = lambda h: pl.ds(h * HALF, HALF)

    ax = Gather4(links, me.ring_x(), lambda c: W.at[0, y, c, zl], lambda c, h: W.at[0, y, c, zl, rows(h)], own[0])
    ay = Gather4(links, me.ring_y(), lambda c: W.at[0, c, :, zl], lambda c, h: W.at[0, c, :, zl, rows(h)])
    by = Gather4(links, me.ring_y(), lambda c: W.at[1, c, x, zl], lambda c, h: W.at[1, c, x, zl, rows(h)], own[1])
    bx = Gather4(links, me.ring_x(), lambda c: W.at[1, :, c, zl], lambda c, h: W.at[1, :, c, zl, rows(h)])
    cx = Gather4(links, me.ring_x(), lambda c: W.at[2, y, c], lambda c, h: W.at[2, y, c, h])
    cy = Gather4(links, me.ring_y(), lambda c: W.at[2, c], lambda c, h: W.at[2, c, :, h])
    dy = Gather4(links, me.ring_y(), lambda c: W.at[3, c, x], lambda c, h: W.at[3, c, x, h])
    dx = Gather4(links, me.ring_x(), lambda c: W.at[3, :, c], lambda c, h: W.at[3, :, c, h])

    zn = {}

    def z_view(t, place, which, h):
        if t == 0:
            return W.at[0, lax.rem(y + place, 4), :, which, rows(h)]
        if t == 1:
            return W.at[1, :, lax.rem(x + place, 4), which, rows(h)]
        return W.at[t, y, x, which, rows(h)]

    def z_begin(t, place, src=None):
        zn[t, place] = links.take(), links.take()
        for h, device in ((0, near_plus), (1, near_minus)):
            view = z_view(t, place, zl, h)
            links.start(zn[t, place][h], view if src is None else src(h), view, device)

    def z_finish(t, place):
        for h, device in ((0, near_plus), (1, near_minus)):
            links.arrived(zn[t, place][h], z_view(t, place, 1 - zl, h), device)

    ax.begin()
    by.begin()
    for t in (2, 3):
        matrix_half = lambda h, t=t: vw.at[rows(h), pl.ds(pl.multiple_of((core * 2 + t - 2) * HEAD, HEAD), HEAD)]
        z_begin(t, 0, matrix_half)

    locals_ = []

    def here(src, dst):
        made = pltpu.make_async_copy(src, dst, local.at[len(locals_)])
        made.start()
        locals_.append(made)

    for t in range(4):
        here(own[t], W.at[t, y, x, zl])
    swaps = []

    def swap(src, dst):
        number = links.take()
        links.start(number, src, dst, partner)
        swaps.append((number, dst))

    theirs = pl.ds(pl.multiple_of((1 - core) * 2048, 2048), 2048)
    swap(sp, SP)
    swap(ss, SS)
    swap(sl, SL)
    swap(resp.at[0], XP.at[pl.ds(0, TOK)])
    swap(prompt.at[0], XP.at[pl.ds(TOK, PRO)])
    swap(q.at[0, :, theirs], QP)
    swap(og.at[0, :, theirs], OP)

    ax.forward()
    by.forward()
    for made in locals_:
        made.wait()
    z_finish(2, 0)
    cx.begin()
    z_finish(3, 0)
    dy.begin()
    ax.finish()
    ay.begin()
    z_begin(0, 0)
    by.finish()
    bx.begin()
    z_begin(1, 0)
    cx.forward()
    dy.forward()
    cx.finish()
    cy.begin()
    dy.finish()
    dx.begin()
    ay.forward()
    z_begin(0, 3)
    z_begin(0, 1)
    bx.forward()
    z_begin(1, 3)
    z_begin(1, 1)
    ay.finish()
    z_begin(0, 2)
    bx.finish()
    z_begin(1, 2)
    cy.forward()
    dx.forward()
    for place in range(4):
        z_finish(0, place)
        z_finish(1, place)
    cy.finish()
    dx.finish()
    for number, landing in swaps:
        links.arrived(number, landing, partner)
    links.drain()
    assert links.used <= GATHER_COPIES


def gather(kw, vw, resp, prompt, q, og, sp, ss, sl):
    return pl.pallas_call(
        gather_kernel,
        out_shape=(
            jax.ShapeDtypeStruct((4, 4, 4, 2, ROWS, HEAD), bf16),
            jax.ShapeDtypeStruct((DEV, WIDTH), bf16),
            jax.ShapeDtypeStruct((TOK, 2048), bf16),
            jax.ShapeDtypeStruct((TOK, 2048), bf16),
            jax.ShapeDtypeStruct((1, 2), jnp.int32),
            jax.ShapeDtypeStruct((1, 2), jnp.int32),
            jax.ShapeDtypeStruct((1, 2), jnp.int32),
        ),
        in_specs=[HBM] * 9,
        out_specs=(HBM,) * 7,
        scratch_shapes=[
            pltpu.SemaphoreType.DMA((GATHER_COPIES,)),
            pltpu.SemaphoreType.DMA((GATHER_COPIES,)),
            pltpu.SemaphoreType.DMA((4,)),
        ],
        compiler_params=remote_params(1),
        name="gather",
    )(kw, vw, resp, prompt, q, og, sp, ss, sl)


K_STEP = 1024


def swap_halves(a):
    return pltpu.roll(a, 64, 1)


def tables_of(starts, cos, sin):
    start = starts[0, 1]
    late = pl.multiple_of(192 - start, 16)
    row = lax.broadcasted_iota(jnp.int32, (TOK, HEAD), 0)
    out = []
    for table in (cos, sin):
        first = table[pl.ds(192, TOK), :]
        second = table[pl.ds(late, TOK), :]
        out.append(jnp.concatenate([jnp.where(row < start, first, second), table[pl.ds(128, PRO), :]], 0))
    return out


def project_kernel(ss, SS, resp, prompt, XP, W, cos, sin, gain, XT, raw, keys, vals, pkv, turns, acc):
    step = pl.program_id(0)
    left = jnp.concatenate([resp[0], prompt[0], XP[...]], 0)
    right = jnp.concatenate([W[t] for t in range(4)], 1)
    part = jnp.dot(left, right, preferred_element_type=f32)
    XT[...] = left.T

    @pl.when(step == 0)
    def _():
        acc[...] = part

    @pl.when(step > 0)
    def _():
        acc[...] += part

    @pl.when(step == pl.num_programs(0) - 1)
    def _():
        for d in range(2):
            c, s = tables_of((ss, SS)[d], cos, sin)
            turns[d, 0], turns[d, 1] = c, s
            core = lax.rem(lax.axis_index("grp") + d, 2)
            for j in range(2):
                k = acc[pl.ds(d * DEV, DEV), pl.ds(j * HEAD, HEAD)]
                raw[j, d] = k
                square = jnp.mean(k * k, axis=1, keepdims=True)
                normed = k * lax.rsqrt(square + 1e-06) * gain[...]
                turned = (normed * c + swap_halves(normed) * s).astype(bf16)
                keys[j, d] = turned
                pkv[j, core] = turned[TOK:]
                v = acc[pl.ds(d * DEV, DEV), pl.ds((2 + j) * HEAD, HEAD)].astype(bf16)
                vals[j, d] = v
                pkv[2 + j, core] = v[TOK:]


def project(ss, SS, resp, prompt, XP, W, cos, sin, gain):
    return pl.pallas_call(
        project_kernel,
        out_shape=(
            jax.ShapeDtypeStruct((WIDTH, 2 * DEV), bf16),
            jax.ShapeDtypeStruct((2, 2, DEV, HEAD), f32),
            jax.ShapeDtypeStruct((2, 2, DEV, HEAD), bf16),
            jax.ShapeDtypeStruct((2, 2, DEV, HEAD), bf16),
            jax.ShapeDtypeStruct((4, 2, PRO, HEAD), bf16),
            jax.ShapeDtypeStruct((2, 2, DEV, HEAD), f32),
        ),
        grid=(WIDTH // K_STEP,),
        in_specs=[
            SMEM,
            SMEM,
            pl.BlockSpec((1, TOK, K_STEP), lambda i: (0, 0, i)),
            pl.BlockSpec((1, PRO, K_STEP), lambda i: (0, 0, i)),
            pl.BlockSpec((DEV, K_STEP), lambda i: (0, i)),
            pl.BlockSpec((4, K_STEP, HEAD), lambda i: (0, i, 0)),
            VMEM,
            VMEM,
            VMEM,
        ],
        out_specs=(pl.BlockSpec((K_STEP, 2 * DEV), lambda i: (i, 0)),) + (VMEM,) * 5,
        scratch_shapes=[pltpu.VMEM((2 * DEV, 512), f32)],
        compiler_params=LOCAL,
        name="project",
    )(ss, SS, resp, prompt, XP, W, cos, sin, gain)


SHARE_COPIES = 8


def share_kernel(pkv, everyone, send, recv, local):
    me = Place()
    ring = me.ring_zh()
    greet(ring[1:])
    links = Links(send, recv)
    own = pltpu.make_async_copy(pkv, everyone.at[me.zh], local)
    own.start()
    going = Gather4(
        links, ring, lambda c: everyone.at[c], lambda c, h: everyone.at[c, pl.ds(2 * h, 2)], pkv
    )
    going.begin()
    going.forward()
    going.finish()
    own.wait()
    links.drain()


def share(pkv):
    return pl.pallas_call(
        share_kernel,
        out_shape=jax.ShapeDtypeStruct((4, 4, 2, PRO, HEAD), bf16),
        in_specs=[VMEM],
        out_specs=VMEM,
        scratch_shapes=[
            pltpu.SemaphoreType.DMA((SHARE_COPIES,)),
            pltpu.SemaphoreType.DMA((SHARE_COPIES,)),
            pltpu.SemaphoreType.DMA,
        ],
        compiler_params=remote_params(2),
        name="share",
    )(pkv)


def attention_kernel(
    sp, ss, sl, SP, SS, SL, owner, everyone, keys, vals, Q, OG, QP, OP,
    QG, RG, PP, probs, slopes, queries, cots, parts,
):
    d, j = pl.program_id(0), pl.program_id(1)

    @pl.when((d == 0) & (j == 0))
    def _():
        parts[...] = jnp.zeros_like(parts)

    def number(own, other, i):
        return jnp.where(d == 0, own[0, i], other[0, i])

    slots = [owner[0, number(sp, SP, i)] for i in range(2)]
    start, lens = number(ss, SS, 1), [number(sl, SL, i) for i in range(2)]
    places = [(lax.div(s, 2), lax.rem(s, 2)) for s in slots]
    K = jnp.concatenate([everyone[zh, j, c] for zh, c in places] + [keys[0, 0, :TOK]], 0)
    V = jnp.concatenate([everyone[zh, 2 + j, c] for zh, c in places] + [vals[0, 0, :TOK]], 0)

    key = lax.broadcasted_iota(jnp.int32, (2 * TOK, TOK), 0)
    row = lax.broadcasted_iota(jnp.int32, (2 * TOK, TOK), 1)
    late = row >= start
    first = jnp.where(late, start, 0)
    end = jnp.where(late, start + lens[1], lens[0])
    from_key = jnp.where(key < TOK, jnp.where(late, PRO, 0), first + TOK)
    to_key = jnp.where(key < TOK, jnp.where(late, TOK, PRO), jnp.minimum(end, row + 1) + TOK)
    bias = jnp.where((key >= from_key) & (key < to_key), 0.0, -1e30)
    bias = jnp.concatenate([bias, bias], 1)
    line = lax.broadcasted_iota(jnp.int32, (TOK, HEAD), 0)
    used = line < jnp.where(line >= start, start + lens[1], lens[0])

    def stack(q, og):
        for h in range(8):
            lanes = pl.ds(h * HEAD, HEAD)
            block = pl.ds(h * TOK, TOK)
            queries[block, :] = q[:, lanes]
            cots[block, :] = jnp.where(used, og[:, lanes].astype(f32), 0.0).astype(bf16)

    pl.when(d == 0)(lambda: stack(Q.at[0], OG.at[0]))
    pl.when(d == 1)(lambda: stack(QP, OP))
    for pair in range(4):
        block = pl.ds(pair * 2 * TOK, 2 * TOK)
        q, cot = queries[block, :], cots[block, :]
        scores = lax.dot_general(K, q, (((1,), (1,)), ((), ())), preferred_element_type=f32)
        scores = scores * SCALE + bias
        top = jnp.max(scores, axis=0, keepdims=True)
        weights = jnp.exp(scores - top)
        prob = weights * (1.0 / jnp.sum(weights, axis=0, keepdims=True))
        probs[:, block] = prob.astype(bf16)
        slope = lax.dot_general(V, cot, (((1,), (1,)), ((), ())), preferred_element_type=f32)
        slope = slope.astype(bf16).astype(f32)
        inner = jnp.sum(slope * prob, axis=0, keepdims=True)
        back = (prob * ((slope - inner) * SCALE)).astype(bf16)
        slopes[:, block] = back
        made = lax.dot_general(
            back, K, (((0,), (0,)), ((), ())), preferred_element_type=f32
        ).astype(bf16)
        for i in range(2):
            QG[0, :, pl.ds((2 * pair + i) * HEAD, HEAD)] = made[i * TOK : (i + 1) * TOK]
    dv = jnp.dot(probs[...], cots[...], preferred_element_type=f32)
    dk = jnp.dot(slopes[...], queries[...], preferred_element_type=f32)
    RG[0, 0, 0] = dk[TOK:].astype(bf16)
    RG[0, 0, 1] = dv[TOK:].astype(bf16)
    for s, (zh, c) in enumerate(places):
        parts[zh, j, c] += dk[s * PRO : (s + 1) * PRO]
        parts[zh, 2 + j, c] += dv[s * PRO : (s + 1) * PRO]

    @pl.when((d == 1) & (j == 1))
    def _():
        PP[...] = parts[...].astype(bf16)


def attention(numbers, everyone, keys, vals, Q, OG, QP, OP):
    core = lambda: lax.rem(lax.axis_index("grp"), 2)
    own = pl.BlockSpec((1, TOK, 1024), lambda d, j: (0, 0, core() * 2 + jnp.maximum(d, j)))
    theirs = pl.BlockSpec((TOK, 1024), lambda d, j: (0, d * j))
    here = pl.BlockSpec((1, 1, DEV, HEAD), lambda d, j: (j, d, 0, 0))
    return pl.pallas_call(
        attention_kernel,
        out_shape=(
            jax.ShapeDtypeStruct((2, TOK, 2048), bf16),
            jax.ShapeDtypeStruct((2, 2, 2, TOK, HEAD), bf16),
            jax.ShapeDtypeStruct((4, 4, 2, PRO, HEAD), bf16),
        ),
        grid=(2, 2),
        in_specs=[SMEM] * 7 + [VMEM, here, here, own, own, theirs, theirs],
        out_specs=(
            pl.BlockSpec((1, TOK, 1024), lambda d, j: (d, 0, j)),
            pl.BlockSpec((1, 1, 2, TOK, HEAD), lambda d, j: (j, d, 0, 0, 0)),
            VMEM,
        ),
        scratch_shapes=[
            pltpu.VMEM((256, 1024), bf16),
            pltpu.VMEM((256, 1024), bf16),
            pltpu.VMEM((1024, HEAD), bf16),
            pltpu.VMEM((1024, HEAD), bf16),
            pltpu.VMEM((4, 4, 2, PRO, HEAD), f32),
        ],
        compiler_params=LOCAL,
        name="attention",
    )(*numbers, everyone, keys, vals, Q, OG, QP, OP)


RETURN_COPIES = 8


def return_kernel(PP, QG, PS, QO, land, send, recv):
    me = Place()
    ring, partner = me.ring_zh(), me.partner()
    greet([ring[1], ring[2], partner])
    links = Links(send, recv)

    def add(dst, terms):
        for i in range(2):
            for d in range(2):
                total = terms[0][i, d].astype(f32)
                for term in terms[1:]:
                    total = total + term[i, d].astype(f32)
                dst[i, d] = total.astype(dst.dtype)

    going = Reduce4(
        links, ring, lambda c, h: PP.at[c, pl.ds(2 * h, 2)], lambda i: land.at[i], add
    )
    going.begin()
    queries = links.take()
    links.start(queries, QG.at[1], QO, partner)
    going.mid()
    going.finish(lambda h: PS.at[pl.ds(2 * h, 2)])
    links.arrived(queries, QO, partner)
    links.drain()


def give_back(PP, QG):
    return pl.pallas_call(
        return_kernel,
        out_shape=(
            jax.ShapeDtypeStruct((4, 2, PRO, HEAD), f32),
            jax.ShapeDtypeStruct((TOK, 2048), bf16),
        ),
        in_specs=[VMEM, HBM],
        out_specs=(VMEM, HBM),
        scratch_shapes=[
            pltpu.VMEM((6, 2, 2, PRO, HEAD), bf16),
            pltpu.SemaphoreType.DMA((RETURN_COPIES,)),
            pltpu.SemaphoreType.DMA((RETURN_COPIES,)),
        ],
        compiler_params=remote_params(3),
        name="give_back",
    )(PP, QG)


SUM_COPIES = 80
I_STEP = 640


def sum_kernel(
    raw, RG, PS, turns, gain, XT, W,
    IG, WG,
    xt, w, w2, grads, theirs, D, one, acc1, two, acc2, near, acc3, three, wg, send, recv, local,
):
    me = Place()
    partner = me.partner()
    near_minus, near_plus = me.near_z()
    ring_x, ring_y, ring_zh = me.ring_x(), me.ring_y(), me.ring_zh()
    fetch = pltpu.make_async_copy(XT, xt, local.at[0])
    fetch.start()
    weights = pltpu.make_async_copy(W, w, local.at[1])
    weights.start()
    greet([*ring_x[1:], *ring_y[1:], *ring_zh[1:], near_minus, near_plus, partner])
    links = Links(send, recv)
    core, zl = me.core, me.zl
    swapped = links.take()
    links.start(swapped, W, w2, partner)

    for d in range(2):
        c, s = turns[d, 0], turns[d, 1]
        whose = core if d == 0 else 1 - core
        rows = pl.ds(d * DEV, DEV)
        for j in range(2):
            cot = jnp.concatenate([RG[j, d, 0].astype(f32), PS[j, whose]], 0)
            turned = (cot * c + swap_halves(cot * s)) * gain[...]
            k = raw[j, d]
            inverse = lax.rsqrt(jnp.mean(k * k, axis=1, keepdims=True) + 1e-06)
            along = jnp.mean(k * turned, axis=1, keepdims=True)
            back = inverse * turned - k * (inverse * inverse * inverse * along)
            grads[rows, pl.ds(j * HEAD, HEAD)] = back.astype(bf16)
            values = jnp.concatenate([RG[j, d, 1], PS[2 + j, whose].astype(bf16)], 0)
            grads[rows, pl.ds((2 + j) * HEAD, HEAD)] = values
    crossed = links.take()
    links.start(crossed, grads.at[pl.ds(DEV, DEV)], theirs, partner)
    fetch.wait()

    def term(y, x, kind):
        rows = pl.ds(pl.multiple_of((y * 4 + x) * 320, 320), 320)
        made = jnp.dot(
            xt[rows, :], grads[:, pl.ds(kind * 256, 256)], preferred_element_type=f32
        ).astype(bf16)
        for j in range(2):
            for h in range(2):
                D[2 * kind + j, y, x, h] = made[h * ROWS : (h + 1) * ROWS, j * HEAD : (j + 1) * HEAD]

    def terms_for(kind, place):
        def body(i, carry):
            if kind == 0:
                term(i, place, 0)
            else:
                term(place, i, 1)
            return carry

        lax.fori_loop(0, 4, body, 0)

    def input_part(i):
        rows = pl.ds(pl.multiple_of(i * I_STEP, I_STEP), I_STEP)
        total = 0.0
        for left, right in ((grads[pl.ds(0, DEV), :], w), (theirs[...], w2)):
            both = jnp.concatenate([right[t, rows, :] for t in range(4)], 1)
            total = total + lax.dot_general(
                left, both, (((1,), (1,)), ((), ())), preferred_element_type=f32
            )
        IG[:, rows] = total.astype(bf16)

    def input_parts(begin, end):
        def body(i, carry):
            input_part(i)
            return carry

        lax.fori_loop(begin, end, body, 0)

    first, second = [], []
    for t in range(4):
        if t < 2:
            part = lambda c, h, t=t: D.at[t, :, c, h]
        else:
            part = lambda c, h, t=t: D.at[t, c, :, h]
        ring = ring_x if t < 2 else ring_y
        other = ring_y if t < 2 else ring_x
        first.append(Reduce4(links, ring, part, lambda i, t=t: one.at[t, i], add_blocks))
        second.append(
            Reduce4(
                links,
                other,
                lambda c, h, t=t: acc1.at[t, c, h],
                lambda i, t=t: two.at[t, i],
                add_block,
            )
        )
    class Wave:
        def __init__(self, n):
            self.n, self.slots = n, (n, 2 + n)
            self.pair = [(links.take(), near_plus), (links.take(), near_minus)]
            self.third = Reduce4(
                links, ring_zh, lambda c, h: acc3.at[n, c, cut[h]], lambda i: three.at[n, i, thirds[i]], add_block
            )
            self.last = Gather4(
                links, ring_zh, lambda c: wg.at[core, n, c], lambda c, h: wg.at[core, n, c, cut[h]]
            )
            self.across = links.take()

        def near_begin(self):
            for kind, (number, device) in enumerate(self.pair):
                links.start(number, acc2.at[self.slots[kind], 1 - zl], near.at[self.n, kind], device)

        def near_finish(self):
            for kind, (number, device) in enumerate(self.pair):
                links.arrived(number, near.at[self.n, kind], device)
                for h in range(2):
                    rows = pl.ds(h * HALF, HALF)
                    add_block(
                        acc3.at[self.n, 2 * kind + h],
                        [acc2.at[self.slots[kind], zl, rows], near.at[self.n, kind, rows]],
                    )

        def third_finish(self):
            self.third.finish(lambda h: wg.at[core, self.n, me.zh, cut[h]])

        def across_begin(self):
            links.start(self.across, wg.at[core, self.n], wg.at[core, self.n], partner)

        def across_finish(self):
            links.arrived(self.across, wg.at[1 - core, self.n], partner)

    cut = (pl.ds(0, 48), pl.ds(48, 32))
    thirds = [cut[h] for h in (0, 1, 1, 0, 0, 1)]
    waves = Wave(0), Wave(1)

    for place in (2, 1, 3, 0):
        for kind, at in ((0, me.x), (1, me.y)):
            terms_for(kind, lax.rem(at + place, 4))
            first[2 * kind].send_for(place)
    first[0].mid()
    first[2].mid()
    first[1].begin()
    first[3].begin()
    weights.wait()
    links.arrived(crossed, theirs, partner)
    links.arrived(swapped, w2, partner)
    input_parts(0, 2)

    def turn(t):
        first[t].finish(lambda h: acc1.at[t, :, h])
        second[t].begin()

    def settle(t):
        second[t].finish(lambda h: acc2.at[t, h])

    turn(0)
    turn(2)
    input_parts(2, 4)
    first[1].mid()
    first[3].mid()
    second[0].mid()
    second[2].mid()
    input_parts(4, 7)
    settle(0)
    settle(2)
    waves[0].near_begin()
    turn(1)
    turn(3)
    waves[0].near_finish()
    waves[0].third.begin()
    input_parts(7, 8)
    second[1].mid()
    second[3].mid()
    waves[0].third.mid()
    settle(1)
    settle(3)
    waves[1].near_begin()
    waves[0].third_finish()
    waves[0].last.begin()
    waves[1].near_finish()
    waves[1].third.begin()
    waves[0].last.forward()
    waves[1].third.mid()
    waves[0].last.finish()
    waves[0].across_begin()
    waves[1].third_finish()
    waves[1].last.begin()
    waves[1].last.forward()
    waves[1].last.finish()
    waves[1].across_begin()
    waves[0].across_finish()
    waves[1].across_finish()
    WG[...] = wg[...]
    links.drain()
    assert links.used <= SUM_COPIES


def sum_terms(raw, RG, PS, turns, gain, XT, W):
    return pl.pallas_call(
        sum_kernel,
        out_shape=(
            jax.ShapeDtypeStruct((DEV, WIDTH), bf16),
            jax.ShapeDtypeStruct((2, 2, 4, HALF, HEAD), bf16),
        ),
        in_specs=[VMEM] * 5 + [HBM] * 2,
        out_specs=(VMEM, VMEM),
        scratch_shapes=[
            pltpu.VMEM((WIDTH, 2 * DEV), bf16),
            pltpu.VMEM((4, WIDTH, HEAD), bf16),
            pltpu.VMEM((4, WIDTH, HEAD), bf16),
            pltpu.VMEM((2 * DEV, 512), bf16),
            pltpu.VMEM((DEV, 512), bf16),
            pltpu.VMEM((4, 4, 4, 2, ROWS, HEAD), bf16),
            pltpu.VMEM((4, 6, 4, ROWS, HEAD), bf16),
            pltpu.VMEM((4, 4, 2, ROWS, HEAD), bf16),
            pltpu.VMEM((4, 6, ROWS, HEAD), bf16),
            pltpu.VMEM((4, 2, ROWS, HEAD), bf16),
            pltpu.VMEM((2, 2, ROWS, HEAD), bf16),
            pltpu.VMEM((2, 4, HALF, HEAD), bf16),
            pltpu.VMEM((2, 6, HALF, HEAD), bf16),
            pltpu.VMEM((2, 2, 4, HALF, HEAD), bf16),
            pltpu.SemaphoreType.DMA((SUM_COPIES,)),
            pltpu.SemaphoreType.DMA((SUM_COPIES,)),
            pltpu.SemaphoreType.DMA((2,)),
        ],
        compiler_params=remote_params(4),
        name="sum_terms",
    )(raw, RG, PS, turns, gain, XT, W)


def put_kernel(IG, WG, QG, QO, resp, prompt, qgrad, kout, vout):
    step = pl.program_id(0)
    core = lax.rem(lax.axis_index("grp"), 2)
    resp[0] = IG[:TOK]
    prompt[0] = IG[TOK:]

    @pl.when(step == core)
    def _():
        qgrad[0] = QG[0]

    @pl.when(step != core)
    def _():
        qgrad[0] = QO[...]

    @pl.when(step == 0)
    def _():
        for c in range(2):
            for j in range(2):
                lanes = pl.ds((2 * c + j) * HEAD, HEAD)
                kout[:, lanes] = WG[c, j, 0]
                vout[:, lanes] = WG[c, j, 1]


def put(IG, WG, QG, QO):
    half = WIDTH // 2
    return pl.pallas_call(
        put_kernel,
        out_shape=(
            jax.ShapeDtypeStruct((1, TOK, WIDTH), bf16),
            jax.ShapeDtypeStruct((1, PRO, WIDTH), bf16),
            jax.ShapeDtypeStruct((1, TOK, 4096), bf16),
            jax.ShapeDtypeStruct((ROWS, 512), bf16),
            jax.ShapeDtypeStruct((ROWS, 512), bf16),
        ),
        grid=(2,),
        in_specs=[
            pl.BlockSpec((DEV, half), lambda i: (0, i)),
            VMEM,
            pl.BlockSpec((1, TOK, 2048), lambda i: (0, 0, 0)),
            VMEM,
        ],
        out_specs=(
            pl.BlockSpec((1, TOK, half), lambda i: (0, 0, i)),
            pl.BlockSpec((1, PRO, half), lambda i: (0, 0, i)),
            pl.BlockSpec((1, TOK, 2048), lambda i: (0, 0, i)),
            VMEM,
            VMEM,
        ),
        compiler_params=LOCAL,
        name="put",
    )(IG, WG, QG, QO)


def local(
    queries, out_grad, resp_in, prompt_in, key_matrix, value_matrix, key_gain, seg_prompt, seg_start, seg_len, owner
):
    cos, sin = rotary_tables()
    gain = key_gain.reshape(1, HEAD)

    W, XP, QP, OP, SP, SS, SL = gather(
        key_matrix, value_matrix, resp_in, prompt_in, queries, out_grad, seg_prompt, seg_start, seg_len
    )
    flat = W.reshape(4, WIDTH, HEAD)
    XT, raw, keys, vals, pkv, turns = project(seg_start, SS, resp_in, prompt_in, XP, flat, cos, sin, gain)
    everyone = share(pkv)
    numbers = (seg_prompt, seg_start, seg_len, SP, SS, SL, owner)
    QG, RG, PP = attention(numbers, everyone, keys, vals, queries, out_grad, QP, OP)
    PS, QO = give_back(PP, QG)
    IG, WG = sum_terms(raw, RG, PS, turns, gain, XT, flat)
    resp, prompt, qgrad, kout, vout = put(IG, WG.reshape(2, 2, 2, ROWS, HEAD), QG, QO)
    return qgrad, resp, prompt, kout, vout


def solution(mesh):
    in_specs = (
        P("fsdp", "grp", None),
        P("fsdp", "grp", None),
        P("fsdp", "grp", None),
        P("fsdp", "grp", None),
        P("fsdp", None),
        P("fsdp", None),
        P(),
        P("fsdp", "grp"),
        P("fsdp", "grp"),
        P("fsdp", "grp"),
        P("fsdp", None),
    )
    out_specs = (
        P("fsdp", "grp", None),
        P("fsdp", "grp", None),
        P("fsdp", "grp", None),
        P("fsdp", None),
        P("fsdp", None),
    )
    return jax.shard_map(local, mesh=mesh, in_specs=in_specs, out_specs=out_specs, check_vma=False)
```

profile of v0, /device:TPU:1, one launch (start us, length us, event | category | flops | bytes accessed | tf_op | source)
XLA Modules:
  0.0 158.4 jit_solution(16577760901167548527)
XLA Ops:
  0.6 38.0 %gather.1 = (bf16[4,4,4,2,160,128]{5,4,3,2,1,0:T(8,128)(2,1)}, bf16[192,5120]{1,0:T(8,128)(2,1)}, bf16[128,2048]{1,0:T(8,128)(2,1)}, bf16[128,2048]{1,0:T(8,128)...) custom-call(bf16[160,512]{1,0:T(8,128)(2,1)} %kw.1, bf16[160,512]{1,0:T(8,128)(2,1)} %vw.1, ...), custom_call_target="tpu_custom_call" | custom-call | tf_op jit(solution)/shard_map/gather/pallas_call | solution.py:327
  38.7 9.5 %project.1 = (bf16[5120,384]{1,0:T(8,128)(2,1)}, f32[2,2,192,128]{3,2,1,0:T(8,128)}, bf16[2,2,192,128]{3,2,1,0:T(8,128)(2,1)}, bf16[2,2,192,128]{3,2,1,0:T(8,128...) custom-call(s32[1,2]{1,0:T(1,128)} %ss.5, s32[1,2]{1,0:T(1,128)} %get-tuple-element.30.SS, ...), custom_call_target="tpu_custom_call" | custom-call | tf_op jit(solution)/shard_map/project/pallas_call | solution.py:404
  48.2 14.2 %share.1.everyone = bf16[4,4,2,64,128]{4,3,2,1,0:T(8,128)(2,1)} custom-call(bf16[4,2,64,128]{3,2,1,0:T(8,128)(2,1)} %get-tuple-element.36.pkv), custom_call_target="tpu_custom_call" | custom-call | tf_op jit(solution)/shard_map/share/pallas_call | solution.py:454
  62.4 11.1 %attention.1 = (bf16[2,128,2048]{2,1,0:T(8,128)(2,1)}, bf16[2,2,2,128,128]{4,3,2,1,0:T(8,128)(2,1)}, bf16[4,4,2,64,128]{4,3,2,1,0:T(8,128)(2,1)}) custom-call(s32[1,2]{1,0:T(1,128)} %sp.3, s32[1,2]{1,0:T(1,128)} %ss.5, s32[1,2]{1,0:T(1,128)} %sl.3, s32[1,2]{1,0:T(1,128)} %get-tuple-element.34.SP, s32[1,2]{1,0:T(1,128)} %get-tuple-element.30.SS, ...), custom_call_target="tpu_custom_call" | custom-call | tf_op jit(solution)/shard_map/attention/pallas_call | solution.py:546
  73.5 16.9 %give_back.1 = (f32[4,2,64,128]{3,2,1,0:T(8,128)}, bf16[128,2048]{1,0:T(8,128)(2,1)}) custom-call(bf16[4,4,2,64,128]{4,3,2,1,0:T(8,128)(2,1)} %get-tuple-element.42.PP, bf16[2,128,2048]{2,1,0:T(8,128)(2,1)} %get-tuple-element.43.QG), custom_call_target="tpu_custom_call" | custom-call | tf_op jit(solution)/shard_map/give_back/pallas_call | solution.py:602
  90.4 64.5 %sum_terms.1 = (bf16[192,5120]{1,0:T(8,128)(2,1)}, bf16[2,2,4,80,128]{4,3,2,1,0:T(8,128)(2,1)}) custom-call(f32[2,2,192,128]{3,2,1,0:T(8,128)} %get-tuple-element.33.raw, bf16[2,2,2,128,128]{4,3,2,1,0:T(8,128)(2,1)} %get-tuple-element.41.RG, f32[4,2,64,128]{3,2,1,0:T(8,128)} %get-tuple-element.44.PS, f32[2,2,192,128]{3,2,1,0:T(8,128)} %get-tuple-element.45.turns, ...), custom_call_target="tpu_custom_call" | custom-call | tf_op jit(solution)/shard_map/sum_terms/pallas_call | solution.py:817
  154.9 3.5 %put.1 = (bf16[1,128,5120]{2,1,0:T(8,128)(2,1)}, bf16[1,64,5120]{2,1,0:T(8,128)(2,1)}, bf16[1,128,4096]{2,1,0:T(8,128)(2,1)}, bf16[160,512]{1,0:T(8,128)(2,1)}, bf16[160,512]{1,0:T(8,128)(2,1)}) custom-call(bf16[192,5120]{1,0:T(8,128)(2,1)} %get-tuple-element.47.IG, bf16[2,2,2,160,128]{4,3,2,1,0:T(8,128)(2,1)} %bitcast.5, ...), custom_call_target="tpu_custom_call" | custom-call | tf_op jit(solution)/shard_map/put/pallas_call | solution.py:874
where the time goes:
time: 159 us; the launch traced here: 158 us
  Pallas kernels  158 us (99%)
    pallas_call x1, Pallas kernels, sum_terms(): pl.pallas_call(sum_kernel, out_shape=(jax.ShapeDtypeStruct((DEV, WIDTH),...  64.5 us
    pallas_call x1, Pallas kernels, gather(): pl.pallas_call(gather_kernel, out_shape=(jax.ShapeDtypeStruct((4, 4, 4, 2...  38 us
    pallas_call x1, Pallas kernels, give_back(): pl.pallas_call(return_kernel, out_shape=(jax.ShapeDtypeStruct((4, 2, PRO,...  16.9 us
    pallas_call x1, Pallas kernels, share(): pl.pallas_call(share_kernel, out_shape=jax.ShapeDtypeStruct((4, 4, 2, PRO...  14.2 us
    pallas_call x1, Pallas kernels, attention(): pl.pallas_call(attention_kernel, out_shape=(jax.ShapeDtypeStruct((2, TOK,...  11.1 us
    pallas_call x1, Pallas kernels, project(): pl.pallas_call(project_kernel, out_shape=(jax.ShapeDtypeStruct((WIDTH, 2...  9.53 us
    pallas_call x1, Pallas kernels, put(): pl.pallas_call(put_kernel, out_shape=(jax.ShapeDtypeStruct((1, TOK, WIDTH...  3.5 us

commit v1 on v0

--- a/solution.py
+++ b/solution.py
@@ -67,6 +67,15 @@
     def near_z(self):
         return self.at(z=lax.rem(self.z + 7, 8)), self.at(z=lax.rem(self.z + 1, 8))
 
+    def first_axis(self, kind):
+        return self.x * (1 - kind) + self.y * kind
+
+    def ring_of(self, kind):
+        def moved(step):
+            return self.at(x=lax.rem(self.x + step * (1 - kind), 4), y=lax.rem(self.y + step * kind, 4))
+
+        return self.first_axis(kind), moved(3), moved(1)
+
     def partner(self):
         return self.at(core=1 - self.core)
 
@@ -193,9 +202,72 @@
     lax.fori_loop(0, dst.shape[0], body, 0)
 
 
-def remote_params(number):
+class Move4:
+    def __init__(self, links, me, XT, XG, relay, zl):
+        self.links, self.me, self.XT, self.XG, self.relay, self.zl = links, me, XT, XG, relay, zl
+        self.place, self.minus, self.plus = me.ring_of(me.core)
+        self.n = [links.take() for _ in range(9)]
+        self.held = [pl.ds(0, 2), pl.ds(2, 2)]
+
+    def from_place(self, steps):
+        return lax.rem(self.place + steps, 4)
+
+    def begin(self):
+        mine = self.XG.at[self.me.core, self.place]
+        jobs = (
+            (0, 2, 0, self.relay.at[0], self.plus),
+            (1, 2, 1, self.relay.at[1], self.minus),
+            (2, 1, None, mine, self.plus),
+            (3, 3, None, mine, self.minus),
+        )
+
+        def start(kind):
+            for n, steps, h, dst, device in jobs:
+                c = self.from_place(steps)
+                rows = pl.ds(0, 4) if h is None else self.held[h]
+                src = self.XT.at[rows, c, self.zl] if kind == 0 else self.XT.at[c, rows, self.zl]
+                self.links.copy(self.n[n], src, dst, device).start()
+
+        pl.when(self.me.core == 0)(lambda: start(0))
+        pl.when(self.me.core == 1)(lambda: start(1))
+        for n, steps, h, dst, device in jobs:
+            self.links.sent.append(self.links.copy(self.n[n], dst, dst, device))
+
+    def forward(self):
+        core, n = self.me.core, self.n
+        self.links.arrived(n[0], self.relay.at[0], self.plus)
+        self.links.start(n[4], self.relay.at[0], self.XG.at[core, self.from_place(3), self.held[0]], self.plus)
+        self.links.arrived(n[1], self.relay.at[1], self.minus)
+        self.links.start(n[5], self.relay.at[1], self.XG.at[core, self.from_place(1), self.held[1]], self.minus)
+
+    def hand_over(self, steps):
+        core, n, partner = self.me.core, self.n, self.me.partner()
+        view = self.XG.at[core, self.from_place(steps)]
+        if steps == 3:
+            self.links.arrived(n[2], view, self.plus)
+        elif steps == 1:
+            self.links.arrived(n[3], view, self.minus)
+        else:
+            c = self.from_place(2)
+            self.links.arrived(n[4], self.XG.at[core, c, self.held[0]], self.plus)
+            self.links.arrived(n[5], self.XG.at[core, c, self.held[1]], self.minus)
+        self.links.start(n[5 + steps], view, view, partner)
+
+    def finish(self):
+        other = 1 - self.me.core
+        for steps in (1, 2, 3):
+            c = lax.rem(self.me.first_axis(other) + steps, 4)
+            self.links.arrived(self.n[5 + steps], self.XG.at[other, c], self.me.partner())
+
+
+X_GATHERED = jax.ShapeDtypeStruct((2, 4, 4, ROWS, 2 * DEV), bf16)
+W_SHAPE = jax.ShapeDtypeStruct((2, 4, 4, 2, ROWS, HEAD), bf16)
+RELAY = pltpu.VMEM((2, 2, ROWS, 2 * DEV), bf16)
+
+
+def remote_params(number, limit=None):
     return pltpu.CompilerParams(
-        collective_id=number, has_side_effects=True, vmem_limit_bytes=VMEM_LIMIT
+        collective_id=number, has_side_effects=True, vmem_limit_bytes=limit or VMEM_LIMIT
     )
 
 
@@ -430,40 +502,52 @@
     )(ss, SS, resp, prompt, XP, W, cos, sin, gain)
 
 
-SHARE_COPIES = 8
-
-
-def share_kernel(pkv, everyone, send, recv, local):
+SHARE_COPIES = 16
+
+
+def share_kernel(pkv, XT, W, everyone, XG, W2, relay, send, recv, local):
     me = Place()
     ring = me.ring_zh()
-    greet(ring[1:])
     links = Links(send, recv)
-    own = pltpu.make_async_copy(pkv, everyone.at[me.zh], local)
-    own.start()
     going = Gather4(
         links, ring, lambda c: everyone.at[c], lambda c, h: everyone.at[c, pl.ds(2 * h, 2)], pkv
     )
+    columns = Move4(links, me, XT, XG, relay, 0)
+    weights = links.take()
+    greet([ring[1], ring[2], columns.minus, columns.plus, me.partner()])
+    own = pltpu.make_async_copy(pkv, everyone.at[me.zh], local)
+    own.start()
     going.begin()
+    columns.begin()
+    links.start(weights, W.at[pl.ds(0, 2)], W2, me.partner())
     going.forward()
+    columns.forward()
+    columns.hand_over(3)
+    columns.hand_over(1)
     going.finish()
+    columns.hand_over(2)
     own.wait()
+    columns.finish()
+    links.arrived(weights, W2, me.partner())
     links.drain()
-
-
-def share(pkv):
+    assert links.used <= SHARE_COPIES
+
+
+def share(pkv, XT, W):
     return pl.pallas_call(
         share_kernel,
-        out_shape=jax.ShapeDtypeStruct((4, 4, 2, PRO, HEAD), bf16),
-        in_specs=[VMEM],
-        out_specs=VMEM,
+        out_shape=(jax.ShapeDtypeStruct((4, 4, 2, PRO, HEAD), bf16), X_GATHERED, W_SHAPE),
+        in_specs=[VMEM, HBM, HBM],
+        out_specs=(VMEM, HBM, HBM),
         scratch_shapes=[
+            RELAY,
             pltpu.SemaphoreType.DMA((SHARE_COPIES,)),
             pltpu.SemaphoreType.DMA((SHARE_COPIES,)),
             pltpu.SemaphoreType.DMA,
         ],
         compiler_params=remote_params(2),
         name="share",
-    )(pkv)
+    )(pkv, XT, W)
 
 
 def attention_kernel(
@@ -569,14 +653,15 @@
     )(*numbers, everyone, keys, vals, Q, OG, QP, OP)
 
 
-RETURN_COPIES = 8
-
-
-def return_kernel(PP, QG, PS, QO, land, send, recv):
+RETURN_COPIES = 24
+
+
+def return_kernel(PP, QG, XT, W, PS, QO, XG, W2, land, relay, send, recv):
     me = Place()
     ring, partner = me.ring_zh(), me.partner()
-    greet([ring[1], ring[2], partner])
     links = Links(send, recv)
+    columns = Move4(links, me, XT, XG, relay, 1)
+    greet([ring[1], ring[2], columns.minus, columns.plus, partner])
 
     def add(dst, terms):
         for i in range(2):
@@ -590,31 +675,43 @@
         links, ring, lambda c, h: PP.at[c, pl.ds(2 * h, 2)], lambda i: land.at[i], add
     )
     going.begin()
-    queries = links.take()
+    columns.begin()
+    queries, weights = links.take(), links.take()
     links.start(queries, QG.at[1], QO, partner)
+    links.start(weights, W.at[pl.ds(2, 2)], W2, partner)
     going.mid()
+    columns.forward()
+    columns.hand_over(3)
+    columns.hand_over(1)
     going.finish(lambda h: PS.at[pl.ds(2 * h, 2)])
+    columns.hand_over(2)
     links.arrived(queries, QO, partner)
+    columns.finish()
+    links.arrived(weights, W2, partner)
     links.drain()
-
-
-def give_back(PP, QG):
+    assert links.used <= RETURN_COPIES
+
+
+def give_back(PP, QG, XT, W):
     return pl.pallas_call(
         return_kernel,
         out_shape=(
             jax.ShapeDtypeStruct((4, 2, PRO, HEAD), f32),
             jax.ShapeDtypeStruct((TOK, 2048), bf16),
+            X_GATHERED,
+            W_SHAPE,
         ),
-        in_specs=[VMEM, HBM],
-        out_specs=(VMEM, HBM),
+        in_specs=[VMEM, HBM, HBM, HBM],
+        out_specs=(VMEM, HBM, HBM, HBM),
         scratch_shapes=[
             pltpu.VMEM((6, 2, 2, PRO, HEAD), bf16),
+            RELAY,
             pltpu.SemaphoreType.DMA((RETURN_COPIES,)),
             pltpu.SemaphoreType.DMA((RETURN_COPIES,)),
         ],
         compiler_params=remote_params(3),
         name="give_back",
-    )(PP, QG)
+    )(PP, QG, XT, W)
 
 
 SUM_COPIES = 80
@@ -622,23 +719,41 @@
 
 
 def sum_kernel(
-    raw, RG, PS, turns, gain, XT, W,
+    raw, RG, PS, turns, gain, XT, XA, XB, W, WA, WB,
     IG, WG,
-    xt, w, w2, grads, theirs, D, one, acc1, two, acc2, near, acc3, three, wg, send, recv, local,
+    xg, w, w2, gg, theirs, acc, acc1, two, acc2, near, acc3, three, wg, send, recv, local,
 ):
     me = Place()
     partner = me.partner()
     near_minus, near_plus = me.near_z()
     ring_x, ring_y, ring_zh = me.ring_x(), me.ring_y(), me.ring_zh()
-    fetch = pltpu.make_async_copy(XT, xt, local.at[0])
-    fetch.start()
-    weights = pltpu.make_async_copy(W, w, local.at[1])
-    weights.start()
+    core, zl = me.core, me.zl
+    place = (me.x, me.y)
+    fetched = {}
+
+    def fetch(name, src, dst):
+        made = pltpu.make_async_copy(src, dst, local.at[sum(len(f) for f in fetched.values())])
+        made.start()
+        fetched.setdefault(name, []).append(made)
+
+    for z in range(2):
+        fetch(0, XT.at[:, me.x, z], xg.at[z, 0, me.x])
+        fetch(0, XT.at[me.y, :, z], xg.at[z, 1, me.y])
+    for steps in (3, 1, 2):
+        for kind in range(2):
+            c = lax.rem(place[kind] + steps, 4)
+            fetch(steps, XA.at[kind, c], xg.at[0, kind, c])
+            fetch(steps, XB.at[kind, c], xg.at[1, kind, c])
+    fetch("w", W, w)
+    fetch("w", WA, w2.at[pl.ds(0, 2)])
+    fetch("w", WB, w2.at[pl.ds(2, 2)])
+
+    def ready(name):
+        for made in fetched[name]:
+            made.wait()
+
     greet([*ring_x[1:], *ring_y[1:], *ring_zh[1:], near_minus, near_plus, partner])
     links = Links(send, recv)
-    core, zl = me.core, me.zl
-    swapped = links.take()
-    links.start(swapped, W, w2, partner)
 
     for d in range(2):
         c, s = turns[d, 0], turns[d, 1]
@@ -651,28 +766,43 @@
             inverse = lax.rsqrt(jnp.mean(k * k, axis=1, keepdims=True) + 1e-06)
             along = jnp.mean(k * turned, axis=1, keepdims=True)
             back = inverse * turned - k * (inverse * inverse * inverse * along)
-            grads[rows, pl.ds(j * HEAD, HEAD)] = back.astype(bf16)
+            gg[0, me.x, rows, pl.ds(j * HEAD, HEAD)] = back.astype(bf16)
             values = jnp.concatenate([RG[j, d, 1], PS[2 + j, whose].astype(bf16)], 0)
-            grads[rows, pl.ds((2 + j) * HEAD, HEAD)] = values
-    crossed = links.take()
-    links.start(crossed, grads.at[pl.ds(DEV, DEV)], theirs, partner)
-    fetch.wait()
-
-    def term(y, x, kind):
-        rows = pl.ds(pl.multiple_of((y * 4 + x) * 320, 320), 320)
-        made = jnp.dot(
-            xt[rows, :], grads[:, pl.ds(kind * 256, 256)], preferred_element_type=f32
-        ).astype(bf16)
-        for j in range(2):
-            for h in range(2):
-                D[2 * kind + j, y, x, h] = made[h * ROWS : (h + 1) * ROWS, j * HEAD : (j + 1) * HEAD]
-
-    def terms_for(kind, place):
+            gg[1, me.y, rows, pl.ds(j * HEAD, HEAD)] = values
+    rounds = []
+    for kind, ring in ((0, ring_x), (1, ring_y)):
+        rounds.append(
+            Gather4(
+                links,
+                ring,
+                lambda c, kind=kind: gg.at[kind, c],
+                lambda c, h, kind=kind: gg.at[kind, c, pl.ds(h * DEV, DEV)],
+            )
+        )
+    for going in rounds:
+        going.begin()
+    crossed = links.take(), links.take()
+    for kind in range(2):
+        links.start(crossed[kind], gg.at[kind, place[kind], pl.ds(DEV, DEV)], theirs.at[kind], partner)
+
+    def terms_of(steps):
         def body(i, carry):
-            if kind == 0:
-                term(i, place, 0)
+            kind, z = lax.div(i, 2), lax.rem(i, 2)
+            c = lax.rem(me.first_axis(kind) + steps, 4)
+            left = jnp.concatenate([xg[z, kind, c, o] for o in range(4)], 0)
+            swapped = 0 if steps == 0 else lax.rem(kind + core, 2)
+            halves = [pl.ds(pl.multiple_of(h * DEV, DEV), DEV) for h in (swapped, 1 - swapped)]
+            right = jnp.concatenate([gg[kind, c, h] for h in halves], 0)
+            made = jnp.dot(left, right, preferred_element_type=f32)
+            if steps != 0:
+                made = made + acc[kind, z]
+            if steps != 2:
+                acc[kind, z] = made
             else:
-                term(place, i, 1)
+                made = made.astype(bf16)
+                for j in range(2):
+                    for o in range(4):
+                        acc1[2 * kind + j, o, z] = made[o * ROWS : (o + 1) * ROWS, j * HEAD : (j + 1) * HEAD]
             return carry
 
         lax.fori_loop(0, 4, body, 0)
@@ -680,8 +810,10 @@
     def input_part(i):
         rows = pl.ds(pl.multiple_of(i * I_STEP, I_STEP), I_STEP)
         total = 0.0
-        for left, right in ((grads[pl.ds(0, DEV), :], w), (theirs[...], w2)):
-            both = jnp.concatenate([right[t, rows, :] for t in range(4)], 1)
+        mine = jnp.concatenate([gg[0, me.x, pl.ds(0, DEV)], gg[1, me.y, pl.ds(0, DEV)]], 1)
+        others = jnp.concatenate([theirs[0], theirs[1]], 1)
+        for left, right in ((mine, w), (others, w2)):
+            both = jnp.concatenate([right[t, pl.ds(i * 4, 4)].reshape(I_STEP, HEAD) for t in range(4)], 1)
             total = total + lax.dot_general(
                 left, both, (((1,), (1,)), ((), ())), preferred_element_type=f32
             )
@@ -694,24 +826,18 @@
 
         lax.fori_loop(begin, end, body, 0)
 
-    first, second = [], []
+    second = []
     for t in range(4):
-        if t < 2:
-            part = lambda c, h, t=t: D.at[t, :, c, h]
-        else:
-            part = lambda c, h, t=t: D.at[t, c, :, h]
-        ring = ring_x if t < 2 else ring_y
-        other = ring_y if t < 2 else ring_x
-        first.append(Reduce4(links, ring, part, lambda i, t=t: one.at[t, i], add_blocks))
         second.append(
             Reduce4(
                 links,
-                other,
+                ring_y if t < 2 else ring_x,
                 lambda c, h, t=t: acc1.at[t, c, h],
                 lambda i, t=t: two.at[t, i],
                 add_block,
             )
         )
+
     class Wave:
         def __init__(self, n):
             self.n, self.slots = n, (n, 2 + n)
@@ -751,59 +877,58 @@
     thirds = [cut[h] for h in (0, 1, 1, 0, 0, 1)]
     waves = Wave(0), Wave(1)
 
-    for place in (2, 1, 3, 0):
-        for kind, at in ((0, me.x), (1, me.y)):
-            terms_for(kind, lax.rem(at + place, 4))
-            first[2 * kind].send_for(place)
-    first[0].mid()
-    first[2].mid()
-    first[1].begin()
-    first[3].begin()
-    weights.wait()
-    links.arrived(crossed, theirs, partner)
-    links.arrived(swapped, w2, partner)
-    input_parts(0, 2)
-
-    def turn(t):
-        first[t].finish(lambda h: acc1.at[t, :, h])
+    ready(0)
+    terms_of(0)
+    for going in rounds:
+        going.forward()
+    ready(3)
+    terms_of(3)
+    ready(1)
+    terms_of(1)
+    for going in rounds:
+        going.finish()
+    ready(2)
+    terms_of(2)
+    for t in (0, 2, 1, 3):
         second[t].begin()
+    ready("w")
+    for kind in range(2):
+        links.arrived(crossed[kind], theirs.at[kind], partner)
 
     def settle(t):
         second[t].finish(lambda h: acc2.at[t, h])
 
-    turn(0)
-    turn(2)
-    input_parts(2, 4)
-    first[1].mid()
-    first[3].mid()
+    input_parts(0, 1)
     second[0].mid()
     second[2].mid()
-    input_parts(4, 7)
+    second[1].mid()
+    second[3].mid()
+    input_parts(1, 2)
     settle(0)
     settle(2)
     waves[0].near_begin()
-    turn(1)
-    turn(3)
+    input_parts(2, 3)
     waves[0].near_finish()
     waves[0].third.begin()
-    input_parts(7, 8)
-    second[1].mid()
-    second[3].mid()
-    waves[0].third.mid()
     settle(1)
     settle(3)
     waves[1].near_begin()
+    waves[0].third.mid()
+    waves[1].near_finish()
+    waves[1].third.begin()
+    input_parts(3, 4)
     waves[0].third_finish()
     waves[0].last.begin()
-    waves[1].near_finish()
-    waves[1].third.begin()
+    waves[1].third.mid()
+    input_parts(4, 5)
     waves[0].last.forward()
-    waves[1].third.mid()
+    waves[1].third_finish()
+    waves[1].last.begin()
+    input_parts(5, 7)
     waves[0].last.finish()
     waves[0].across_begin()
-    waves[1].third_finish()
-    waves[1].last.begin()
     waves[1].last.forward()
+    input_parts(7, 8)
     waves[1].last.finish()
     waves[1].across_begin()
     waves[0].across_finish()
@@ -813,23 +938,22 @@
     assert links.used <= SUM_COPIES
 
 
-def sum_terms(raw, RG, PS, turns, gain, XT, W):
+def sum_terms(raw, RG, PS, turns, gain, XT, XA, XB, W, WA, WB):
     return pl.pallas_call(
         sum_kernel,
         out_shape=(
             jax.ShapeDtypeStruct((DEV, WIDTH), bf16),
             jax.ShapeDtypeStruct((2, 2, 4, HALF, HEAD), bf16),
         ),
-        in_specs=[VMEM] * 5 + [HBM] * 2,
+        in_specs=[VMEM] * 5 + [HBM] * 6,
         out_specs=(VMEM, VMEM),
         scratch_shapes=[
-            pltpu.VMEM((WIDTH, 2 * DEV), bf16),
-            pltpu.VMEM((4, WIDTH, HEAD), bf16),
-            pltpu.VMEM((4, WIDTH, HEAD), bf16),
-            pltpu.VMEM((2 * DEV, 512), bf16),
-            pltpu.VMEM((DEV, 512), bf16),
-            pltpu.VMEM((4, 4, 4, 2, ROWS, HEAD), bf16),
-            pltpu.VMEM((4, 6, 4, ROWS, HEAD), bf16),
+            pltpu.VMEM((2, 2, 4, 4, ROWS, 2 * DEV), bf16),
+            pltpu.VMEM((4, 32, ROWS, HEAD), bf16),
+            pltpu.VMEM((4, 32, ROWS, HEAD), bf16),
+            pltpu.VMEM((2, 4, 2 * DEV, 256), bf16),
+            pltpu.VMEM((2, DEV, 256), bf16),
+            pltpu.VMEM((2, 2, 4 * ROWS, 256), f32),
             pltpu.VMEM((4, 4, 2, ROWS, HEAD), bf16),
             pltpu.VMEM((4, 6, ROWS, HEAD), bf16),
             pltpu.VMEM((4, 2, ROWS, HEAD), bf16),
@@ -839,11 +963,11 @@
             pltpu.VMEM((2, 2, 4, HALF, HEAD), bf16),
             pltpu.SemaphoreType.DMA((SUM_COPIES,)),
             pltpu.SemaphoreType.DMA((SUM_COPIES,)),
-            pltpu.SemaphoreType.DMA((2,)),
+            pltpu.SemaphoreType.DMA((20,)),
         ],
         compiler_params=remote_params(4),
         name="sum_terms",
-    )(raw, RG, PS, turns, gain, XT, W)
+    )(raw, RG, PS, turns, gain, XT, XA, XB, W, WA, WB)
 
 
 def put_kernel(IG, WG, QG, QO, resp, prompt, qgrad, kout, vout):
@@ -910,11 +1034,13 @@
     )
     flat = W.reshape(4, WIDTH, HEAD)
     XT, raw, keys, vals, pkv, turns = project(seg_start, SS, resp_in, prompt_in, XP, flat, cos, sin, gain)
-    everyone = share(pkv)
+    XT = XT.reshape(4, 4, 2, ROWS, 2 * DEV)
+    everyone, XA, WA = share(pkv, XT, W)
     numbers = (seg_prompt, seg_start, seg_len, SP, SS, SL, owner)
     QG, RG, PP = attention(numbers, everyone, keys, vals, queries, out_grad, QP, OP)
-    PS, QO = give_back(PP, QG)
-    IG, WG = sum_terms(raw, RG, PS, turns, gain, XT, flat)
+    PS, QO, XB, WB = give_back(PP, QG, XT, W)
+    pieces = [a.reshape(-1, 32, ROWS, HEAD) for a in (W, WA, WB)]
+    IG, WG = sum_terms(raw, RG, PS, turns, gain, XT, XA, XB, *pieces)
     resp, prompt, qgrad, kout, vout = put(IG, WG.reshape(2, 2, 2, ROWS, HEAD), QG, QO)
     return qgrad, resp, prompt, kout, vout
 

time: 159 us -> 158 us (level)
    pallas_call x1, Pallas kernels: 64.5 us -> 50.8 us  [sum_terms(): pl.pallas_call(sum_kernel, out_shape=(jax.ShapeDtypeStruct((DEV, WIDTH),...]
    pallas_call x1, Pallas kernels: 14.2 us -> 23.7 us  [share(): pl.pallas_call(share_kernel, out_shape=(jax.ShapeDtypeStruct((4, 4, 2, PR...]
    pallas_call x1, Pallas kernels: 16.9 us -> 20 us  [give_back(): pl.pallas_call(return_kernel, out_shape=(jax.ShapeDtypeStruct((4, 2, PRO,...]
where the time goes in v1:
time: 158 us; the launch traced here: 157 us
  Pallas kernels  157 us (99%)
    pallas_call x1, Pallas kernels, sum_terms(): pl.pallas_call(sum_kernel, out_shape=(jax.ShapeDtypeStruct((DEV, WIDTH),...  50.8 us
    pallas_call x1, Pallas kernels, gather(): pl.pallas_call(gather_kernel, out_shape=(jax.ShapeDtypeStruct((4, 4, 4, 2...  38 us
    pallas_call x1, Pallas kernels, share(): pl.pallas_call(share_kernel, out_shape=(jax.ShapeDtypeStruct((4, 4, 2, PR...  23.7 us
    pallas_call x1, Pallas kernels, give_back(): pl.pallas_call(return_kernel, out_shape=(jax.ShapeDtypeStruct((4, 2, PRO,...  20 us
    pallas_call x1, Pallas kernels, attention(): pl.pallas_call(attention_kernel, out_shape=(jax.ShapeDtypeStruct((2, TOK,...  11.1 us
    pallas_call x1, Pallas kernels, project(): pl.pallas_call(project_kernel, out_shape=(jax.ShapeDtypeStruct((WIDTH, 2...  9.53 us
    pallas_call x1, Pallas kernels, put(): pl.pallas_call(put_kernel, out_shape=(jax.ShapeDtypeStruct((1, TOK, WIDTH...  3.5 us

profile of v1, /device:TPU:1, one launch (start us, length us, event | category | flops | bytes accessed | tf_op | source)
XLA Modules:
  0.0 157.3 jit_solution(1749798377493991196)
XLA Ops:
  0.6 38.0 %gather.1 = (bf16[4,4,4,2,160,128]{5,4,3,2,1,0:T(8,128)(2,1)}, bf16[192,5120]{1,0:T(8,128)(2,1)}, bf16[128,2048]{1,0:T(8,128)(2,1)}, bf16[128,2048]{1,0:T(8,128)...) custom-call(bf16[160,512]{1,0:T(8,128)(2,1)} %kw.1, bf16[160,512]{1,0:T(8,128)(2,1)} %vw.1, ...), custom_call_target="tpu_custom_call" | custom-call | tf_op jit(solution)/shard_map/gather/pallas_call | solution.py:399
  38.7 9.5 %project.1 = (bf16[5120,384]{1,0:T(8,128)(2,1)}, f32[2,2,192,128]{3,2,1,0:T(8,128)}, bf16[2,2,192,128]{3,2,1,0:T(8,128)(2,1)}, bf16[2,2,192,128]{3,2,1,0:T(8,128...) custom-call(s32[1,2]{1,0:T(1,128)} %ss.5, s32[1,2]{1,0:T(1,128)} %get-tuple-element.35.SS, ...), custom_call_target="tpu_custom_call" | custom-call | tf_op jit(solution)/shard_map/project/pallas_call | solution.py:476
  48.2 23.7 %share.1 = (bf16[4,4,2,64,128]{4,3,2,1,0:T(8,128)(2,1)}, bf16[2,4,4,160,384]{4,3,2,1,0:T(8,128)(2,1)}, bf16[2,4,4,2,160,128]{5,4,3,2,1,0:T(8,128)(2,1)}) custom-call(bf16[4,2,64,128]{3,2,1,0:T(8,128)(2,1)} %get-tuple-element.41.pkv, bf16[4,4,2,160,384]{4,3,2,1,0:T(8,128)(2,1)} %bitcast.9, bf16[4,4,4,2,160,128]{5,4,3,2,1,0:T(8,128)(2,1)} %get-tuple-element.37.W), custom_call_target="tpu_custom_call" | custom-call | tf_op jit(solution)/shard_map/share/pallas_call | solution.py:537
  71.9 11.1 %attention.1 = (bf16[2,128,2048]{2,1,0:T(8,128)(2,1)}, bf16[2,2,2,128,128]{4,3,2,1,0:T(8,128)(2,1)}, bf16[4,4,2,64,128]{4,3,2,1,0:T(8,128)(2,1)}) custom-call(s32[1,2]{1,0:T(1,128)} %sp.3, s32[1,2]{1,0:T(1,128)} %ss.5, s32[1,2]{1,0:T(1,128)} %sl.3, s32[1,2]{1,0:T(1,128)} %get-tuple-element.39.SP, s32[1,2]{1,0:T(1,128)} %get-tuple-element.35.SS, ...), custom_call_target="tpu_custom_call" | custom-call | tf_op jit(solution)/shard_map/attention/pallas_call | solution.py:630
  83.0 20.0 %give_back.1 = (f32[4,2,64,128]{3,2,1,0:T(8,128)}, bf16[128,2048]{1,0:T(8,128)(2,1)}, bf16[2,4,4,160,384]{4,3,2,1,0:T(8,128)(2,1)}, bf16[2,4,4,2,160,128]{5,4,3,2,1,0:T(8,128)(2,1)}) custom-call(bf16[4,4,2,64,128]{4,3,2,1,0:T(8,128)(2,1)} %get-tuple-element.49.PP, bf16[2,128,2048]{2,1,0:T(8,128)(2,1)} %get-tuple-element.50.QG, ...), custom_call_target="tpu_custom_call" | custom-call | tf_op jit(solution)/shard_map/give_back/pallas_call | solution.py:696
  103.1 50.8 %sum_terms.1 = (bf16[192,5120]{1,0:T(8,128)(2,1)}, bf16[2,2,4,80,128]{4,3,2,1,0:T(8,128)(2,1)}) custom-call(f32[2,2,192,128]{3,2,1,0:T(8,128)} %get-tuple-element.38.raw, bf16[2,2,2,128,128]{4,3,2,1,0:T(8,128)(2,1)} %get-tuple-element.48.RG, f32[4,2,64,128]{3,2,1,0:T(8,128)} %get-tuple-element.51.PS, f32[2,2,192,128]{3,2,1,0:T(8,128)} %get-tuple-element.52.turns, ...), custom_call_target="tpu_custom_call" | custom-call | tf_op jit(solution)/shard_map/sum_terms/pallas_call | solution.py:942
  153.9 3.5 %put.1 = (bf16[1,128,5120]{2,1,0:T(8,128)(2,1)}, bf16[1,64,5120]{2,1,0:T(8,128)(2,1)}, bf16[1,128,4096]{2,1,0:T(8,128)(2,1)}, bf16[160,512]{1,0:T(8,128)(2,1)}, bf16[160,512]{1,0:T(8,128)(2,1)}) custom-call(bf16[192,5120]{1,0:T(8,128)(2,1)} %get-tuple-element.57.IG, bf16[2,2,2,160,128]{4,3,2,1,0:T(8,128)(2,1)} %bitcast.14, ...), custom_call_target="tpu_custom_call" | custom-call | tf_op jit(solution)/shard_map/put/pallas_call | solution.py:998

commit v2 on v1

--- a/solution.py
+++ b/solution.py
@@ -258,11 +258,6 @@
         for steps in (1, 2, 3):
             c = lax.rem(self.me.first_axis(other) + steps, 4)
             self.links.arrived(self.n[5 + steps], self.XG.at[other, c], self.me.partner())
-
-
-X_GATHERED = jax.ShapeDtypeStruct((2, 4, 4, ROWS, 2 * DEV), bf16)
-W_SHAPE = jax.ShapeDtypeStruct((2, 4, 4, 2, ROWS, HEAD), bf16)
-RELAY = pltpu.VMEM((2, 2, ROWS, 2 * DEV), bf16)
 
 
 def remote_params(number, limit=None):
@@ -502,166 +497,129 @@
     )(ss, SS, resp, prompt, XP, W, cos, sin, gain)
 
 
-SHARE_COPIES = 16
-
-
-def share_kernel(pkv, XT, W, everyone, XG, W2, relay, send, recv, local):
+ATTEND_COPIES = 40
+
+
+def attend_kernel(
+    sp, ss, sl, SP, SS, SL, owner, pkv, keys, vals, q, og, QP, OP, XT, W,
+    QG, QO, RG, PS, XG, W2,
+    everyone, queries, cots, rows_q, rows_g, probs, slopes, made_q, parts, PP, land, relay, send, recv, local,
+):
     me = Place()
+    core, partner = me.core, me.partner()
     ring = me.ring_zh()
     links = Links(send, recv)
-    going = Gather4(
-        links, ring, lambda c: everyone.at[c], lambda c, h: everyone.at[c, pl.ds(2 * h, 2)], pkv
-    )
-    columns = Move4(links, me, XT, XG, relay, 0)
-    weights = links.take()
-    greet([ring[1], ring[2], columns.minus, columns.plus, me.partner()])
-    own = pltpu.make_async_copy(pkv, everyone.at[me.zh], local)
-    own.start()
-    going.begin()
-    columns.begin()
-    links.start(weights, W.at[pl.ds(0, 2)], W2, me.partner())
-    going.forward()
-    columns.forward()
-    columns.hand_over(3)
-    columns.hand_over(1)
-    going.finish()
-    columns.hand_over(2)
-    own.wait()
-    columns.finish()
-    links.arrived(weights, W2, me.partner())
-    links.drain()
-    assert links.used <= SHARE_COPIES
-
-
-def share(pkv, XT, W):
-    return pl.pallas_call(
-        share_kernel,
-        out_shape=(jax.ShapeDtypeStruct((4, 4, 2, PRO, HEAD), bf16), X_GATHERED, W_SHAPE),
-        in_specs=[VMEM, HBM, HBM],
-        out_specs=(VMEM, HBM, HBM),
-        scratch_shapes=[
-            RELAY,
-            pltpu.SemaphoreType.DMA((SHARE_COPIES,)),
-            pltpu.SemaphoreType.DMA((SHARE_COPIES,)),
-            pltpu.SemaphoreType.DMA,
-        ],
-        compiler_params=remote_params(2),
-        name="share",
-    )(pkv, XT, W)
-
-
-def attention_kernel(
-    sp, ss, sl, SP, SS, SL, owner, everyone, keys, vals, Q, OG, QP, OP,
-    QG, RG, PP, probs, slopes, queries, cots, parts,
-):
-    d, j = pl.program_id(0), pl.program_id(1)
-
-    @pl.when((d == 0) & (j == 0))
-    def _():
-        parts[...] = jnp.zeros_like(parts)
-
-    def number(own, other, i):
-        return jnp.where(d == 0, own[0, i], other[0, i])
-
-    slots = [owner[0, number(sp, SP, i)] for i in range(2)]
-    start, lens = number(ss, SS, 1), [number(sl, SL, i) for i in range(2)]
-    places = [(lax.div(s, 2), lax.rem(s, 2)) for s in slots]
-    K = jnp.concatenate([everyone[zh, j, c] for zh, c in places] + [keys[0, 0, :TOK]], 0)
-    V = jnp.concatenate([everyone[zh, 2 + j, c] for zh, c in places] + [vals[0, 0, :TOK]], 0)
-
-    key = lax.broadcasted_iota(jnp.int32, (2 * TOK, TOK), 0)
-    row = lax.broadcasted_iota(jnp.int32, (2 * TOK, TOK), 1)
-    late = row >= start
-    first = jnp.where(late, start, 0)
-    end = jnp.where(late, start + lens[1], lens[0])
-    from_key = jnp.where(key < TOK, jnp.where(late, PRO, 0), first + TOK)
-    to_key = jnp.where(key < TOK, jnp.where(late, TOK, PRO), jnp.minimum(end, row + 1) + TOK)
-    bias = jnp.where((key >= from_key) & (key < to_key), 0.0, -1e30)
-    bias = jnp.concatenate([bias, bias], 1)
-    line = lax.broadcasted_iota(jnp.int32, (TOK, HEAD), 0)
-    used = line < jnp.where(line >= start, start + lens[1], lens[0])
-
-    def stack(q, og):
+    out = Gather4(links, ring, lambda c: everyone.at[c], lambda c, h: everyone.at[c, pl.ds(2 * h, 2)], pkv)
+    columns = [Move4(links, me, XT, XG.at[z], relay.at[z], z) for z in range(2)]
+    weights, swapped = links.take(), links.take()
+    greet([ring[1], ring[2], columns[0].minus, columns[0].plus, partner])
+    mine = pl.ds(pl.multiple_of(core * 2048, 2048), 2048)
+    locals_ = []
+    out.begin()
+    for src, dst in (
+        (pkv, everyone.at[me.zh]),
+        (q.at[0, :, mine], rows_q.at[0]),
+        (og.at[0, :, mine], rows_g.at[0]),
+        (QP, rows_q.at[1]),
+        (OP, rows_g.at[1]),
+    ):
+        made = pltpu.make_async_copy(src, dst, local.at[len(locals_)])
+        made.start()
+        locals_.append(made)
+    columns[0].begin()
+    columns[1].begin()
+    links.start(weights, W, W2, partner)
+    parts[...] = jnp.zeros_like(parts)
+    out.forward()
+    columns[0].forward()
+    out.finish()
+    for made in locals_:
+        made.wait()
+
+    def attend(i, carry):
+        d, j = lax.div(i, 2), lax.rem(i, 2)
+
+        def number(own, other, n):
+            return jnp.where(d == 0, own[0, n], other[0, n])
+
+        def slot_of(prompt):
+            slot = 0
+            for p in range(8):
+                slot = slot + jnp.where(prompt == p, owner[0, p], 0)
+            return slot
+
+        slots = [slot_of(number(sp, SP, n)) for n in range(2)]
+        start, lens = number(ss, SS, 1), [number(sl, SL, n) for n in range(2)]
+        chosen = [[jnp.where(s == slot, 1.0, 0.0) for slot in range(8)] for s in slots]
+
+        def pick(t, own):
+            blocks = []
+            for one in chosen:
+                total = 0.0
+                for slot in range(8):
+                    total = total + everyone[slot // 2, t, slot % 2].astype(f32) * one[slot]
+                blocks.append(total.astype(bf16))
+            return jnp.concatenate(blocks + [own], 0)
+
+        K = pick(j, keys[j, d, :TOK])
+        V = pick(2 + j, vals[j, d, :TOK])
+
+        key = lax.broadcasted_iota(jnp.int32, (2 * TOK, TOK), 0)
+        row = lax.broadcasted_iota(jnp.int32, (2 * TOK, TOK), 1)
+        late = row >= start
+        first = jnp.where(late, start, 0)
+        end = jnp.where(late, start + lens[1], lens[0])
+        from_key = jnp.where(key < TOK, jnp.where(late, PRO, 0), first + TOK)
+        to_key = jnp.where(key < TOK, jnp.where(late, TOK, PRO), jnp.minimum(end, row + 1) + TOK)
+        bias = jnp.where((key >= from_key) & (key < to_key), 0.0, -1e30)
+        bias = jnp.concatenate([bias, bias], 1)
+        line = lax.broadcasted_iota(jnp.int32, (TOK, HEAD), 0)
+        used = line < jnp.where(line >= start, start + lens[1], lens[0])
+
+        def lanes(h):
+            return pl.ds(pl.multiple_of(j * 1024 + h * HEAD, HEAD), HEAD)
+
         for h in range(8):
-            lanes = pl.ds(h * HEAD, HEAD)
             block = pl.ds(h * TOK, TOK)
-            queries[block, :] = q[:, lanes]
-            cots[block, :] = jnp.where(used, og[:, lanes].astype(f32), 0.0).astype(bf16)
-
-    pl.when(d == 0)(lambda: stack(Q.at[0], OG.at[0]))
-    pl.when(d == 1)(lambda: stack(QP, OP))
-    for pair in range(4):
-        block = pl.ds(pair * 2 * TOK, 2 * TOK)
-        q, cot = queries[block, :], cots[block, :]
-        scores = lax.dot_general(K, q, (((1,), (1,)), ((), ())), preferred_element_type=f32)
-        scores = scores * SCALE + bias
-        top = jnp.max(scores, axis=0, keepdims=True)
-        weights = jnp.exp(scores - top)
-        prob = weights * (1.0 / jnp.sum(weights, axis=0, keepdims=True))
-        probs[:, block] = prob.astype(bf16)
-        slope = lax.dot_general(V, cot, (((1,), (1,)), ((), ())), preferred_element_type=f32)
-        slope = slope.astype(bf16).astype(f32)
-        inner = jnp.sum(slope * prob, axis=0, keepdims=True)
-        back = (prob * ((slope - inner) * SCALE)).astype(bf16)
-        slopes[:, block] = back
-        made = lax.dot_general(
-            back, K, (((0,), (0,)), ((), ())), preferred_element_type=f32
-        ).astype(bf16)
-        for i in range(2):
-            QG[0, :, pl.ds((2 * pair + i) * HEAD, HEAD)] = made[i * TOK : (i + 1) * TOK]
-    dv = jnp.dot(probs[...], cots[...], preferred_element_type=f32)
-    dk = jnp.dot(slopes[...], queries[...], preferred_element_type=f32)
-    RG[0, 0, 0] = dk[TOK:].astype(bf16)
-    RG[0, 0, 1] = dv[TOK:].astype(bf16)
-    for s, (zh, c) in enumerate(places):
-        parts[zh, j, c] += dk[s * PRO : (s + 1) * PRO]
-        parts[zh, 2 + j, c] += dv[s * PRO : (s + 1) * PRO]
-
-    @pl.when((d == 1) & (j == 1))
-    def _():
-        PP[...] = parts[...].astype(bf16)
-
-
-def attention(numbers, everyone, keys, vals, Q, OG, QP, OP):
-    core = lambda: lax.rem(lax.axis_index("grp"), 2)
-    own = pl.BlockSpec((1, TOK, 1024), lambda d, j: (0, 0, core() * 2 + jnp.maximum(d, j)))
-    theirs = pl.BlockSpec((TOK, 1024), lambda d, j: (0, d * j))
-    here = pl.BlockSpec((1, 1, DEV, HEAD), lambda d, j: (j, d, 0, 0))
-    return pl.pallas_call(
-        attention_kernel,
-        out_shape=(
-            jax.ShapeDtypeStruct((2, TOK, 2048), bf16),
-            jax.ShapeDtypeStruct((2, 2, 2, TOK, HEAD), bf16),
-            jax.ShapeDtypeStruct((4, 4, 2, PRO, HEAD), bf16),
-        ),
-        grid=(2, 2),
-        in_specs=[SMEM] * 7 + [VMEM, here, here, own, own, theirs, theirs],
-        out_specs=(
-            pl.BlockSpec((1, TOK, 1024), lambda d, j: (d, 0, j)),
-            pl.BlockSpec((1, 1, 2, TOK, HEAD), lambda d, j: (j, d, 0, 0, 0)),
-            VMEM,
-        ),
-        scratch_shapes=[
-            pltpu.VMEM((256, 1024), bf16),
-            pltpu.VMEM((256, 1024), bf16),
-            pltpu.VMEM((1024, HEAD), bf16),
-            pltpu.VMEM((1024, HEAD), bf16),
-            pltpu.VMEM((4, 4, 2, PRO, HEAD), f32),
-        ],
-        compiler_params=LOCAL,
-        name="attention",
-    )(*numbers, everyone, keys, vals, Q, OG, QP, OP)
-
-
-RETURN_COPIES = 24
-
-
-def return_kernel(PP, QG, XT, W, PS, QO, XG, W2, land, relay, send, recv):
-    me = Place()
-    ring, partner = me.ring_zh(), me.partner()
-    links = Links(send, recv)
-    columns = Move4(links, me, XT, XG, relay, 1)
-    greet([ring[1], ring[2], columns.minus, columns.plus, partner])
+            queries[block, :] = rows_q[d, :, lanes(h)]
+            cots[block, :] = jnp.where(used, rows_g[d, :, lanes(h)].astype(f32), 0.0).astype(bf16)
+        for pair in range(4):
+            block = pl.ds(pair * 2 * TOK, 2 * TOK)
+            query, cot = queries[block, :], cots[block, :]
+            scores = lax.dot_general(K, query, (((1,), (1,)), ((), ())), preferred_element_type=f32)
+            scores = scores * SCALE + bias
+            top = jnp.max(scores, axis=0, keepdims=True)
+            exps = jnp.exp(scores - top)
+            prob = exps * (1.0 / jnp.sum(exps, axis=0, keepdims=True))
+            probs[:, block] = prob.astype(bf16)
+            slope = lax.dot_general(V, cot, (((1,), (1,)), ((), ())), preferred_element_type=f32)
+            slope = slope.astype(bf16).astype(f32)
+            inner = jnp.sum(slope * prob, axis=0, keepdims=True)
+            back = (prob * ((slope - inner) * SCALE)).astype(bf16)
+            slopes[:, block] = back
+            grad = lax.dot_general(
+                back, K, (((0,), (0,)), ((), ())), preferred_element_type=f32
+            ).astype(bf16)
+            for n in range(2):
+                made_q[d, :, lanes(2 * pair + n)] = grad[n * TOK : (n + 1) * TOK]
+        dv = jnp.dot(probs[...], cots[...], preferred_element_type=f32)
+        dk = jnp.dot(slopes[...], queries[...], preferred_element_type=f32)
+        RG[j, d, 0] = dk[TOK:].astype(bf16)
+        RG[j, d, 1] = dv[TOK:].astype(bf16)
+        for slot in range(8):
+            for t, grad in ((j, dk), (2 + j, dv)):
+                parts[slot // 2, t, slot % 2] += (
+                    grad[:PRO] * chosen[0][slot] + grad[PRO:TOK] * chosen[1][slot]
+                )
+        return carry
+
+    lax.fori_loop(2, 4, attend, 0)
+    links.start(swapped, made_q.at[1], QO, partner)
+    columns[1].forward()
+    for steps in (3, 1, 2):
+        columns[0].hand_over(steps)
+    lax.fori_loop(0, 2, attend, 0)
+    PP[...] = parts[...].astype(bf16)
 
     def add(dst, terms):
         for i in range(2):
@@ -671,47 +629,54 @@
                     total = total + term[i, d].astype(f32)
                 dst[i, d] = total.astype(dst.dtype)
 
-    going = Reduce4(
-        links, ring, lambda c, h: PP.at[c, pl.ds(2 * h, 2)], lambda i: land.at[i], add
-    )
-    going.begin()
-    columns.begin()
-    queries, weights = links.take(), links.take()
-    links.start(queries, QG.at[1], QO, partner)
-    links.start(weights, W.at[pl.ds(2, 2)], W2, partner)
-    going.mid()
-    columns.forward()
-    columns.hand_over(3)
-    columns.hand_over(1)
-    going.finish(lambda h: PS.at[pl.ds(2 * h, 2)])
-    columns.hand_over(2)
-    links.arrived(queries, QO, partner)
-    columns.finish()
+    home = Reduce4(links, ring, lambda c, h: PP.at[c, pl.ds(2 * h, 2)], lambda i: land.at[i], add)
+    home.begin()
+    for steps in (3, 1, 2):
+        columns[1].hand_over(steps)
+    QG[...] = made_q[0]
+    home.mid()
+    home.finish(lambda h: PS.at[pl.ds(2 * h, 2)])
+    columns[0].finish()
+    columns[1].finish()
     links.arrived(weights, W2, partner)
+    links.arrived(swapped, QO, partner)
     links.drain()
-    assert links.used <= RETURN_COPIES
-
-
-def give_back(PP, QG, XT, W):
+    assert links.used <= ATTEND_COPIES
+
+
+def attend(numbers, pkv, keys, vals, q, og, QP, OP, XT, W):
     return pl.pallas_call(
-        return_kernel,
+        attend_kernel,
         out_shape=(
+            jax.ShapeDtypeStruct((TOK, 2048), bf16),
+            jax.ShapeDtypeStruct((TOK, 2048), bf16),
+            jax.ShapeDtypeStruct((2, 2, 2, TOK, HEAD), bf16),
             jax.ShapeDtypeStruct((4, 2, PRO, HEAD), f32),
-            jax.ShapeDtypeStruct((TOK, 2048), bf16),
-            X_GATHERED,
-            W_SHAPE,
+            jax.ShapeDtypeStruct((2, 2, 4, 4, ROWS, 2 * DEV), bf16),
+            jax.ShapeDtypeStruct((4, 4, 4, 2, ROWS, HEAD), bf16),
         ),
-        in_specs=[VMEM, HBM, HBM, HBM],
-        out_specs=(VMEM, HBM, HBM, HBM),
+        in_specs=[SMEM] * 7 + [VMEM] * 3 + [HBM] * 6,
+        out_specs=(VMEM, HBM, VMEM, VMEM, HBM, HBM),
         scratch_shapes=[
+            pltpu.VMEM((4, 4, 2, PRO, HEAD), bf16),
+            pltpu.VMEM((1024, HEAD), bf16),
+            pltpu.VMEM((1024, HEAD), bf16),
+            pltpu.VMEM((2, TOK, 2048), bf16),
+            pltpu.VMEM((2, TOK, 2048), bf16),
+            pltpu.VMEM((256, 1024), bf16),
+            pltpu.VMEM((256, 1024), bf16),
+            pltpu.VMEM((2, TOK, 2048), bf16),
+            pltpu.VMEM((4, 4, 2, PRO, HEAD), f32),
+            pltpu.VMEM((4, 4, 2, PRO, HEAD), bf16),
             pltpu.VMEM((6, 2, 2, PRO, HEAD), bf16),
-            RELAY,
-            pltpu.SemaphoreType.DMA((RETURN_COPIES,)),
-            pltpu.SemaphoreType.DMA((RETURN_COPIES,)),
+            pltpu.VMEM((2, 2, 2, ROWS, 2 * DEV), bf16),
+            pltpu.SemaphoreType.DMA((ATTEND_COPIES,)),
+            pltpu.SemaphoreType.DMA((ATTEND_COPIES,)),
+            pltpu.SemaphoreType.DMA((5,)),
         ],
-        compiler_params=remote_params(3),
-        name="give_back",
-    )(PP, QG, XT, W)
+        compiler_params=remote_params(2),
+        name="attend",
+    )(*numbers, pkv, keys, vals, q, og, QP, OP, XT, W)
 
 
 SUM_COPIES = 80
@@ -719,7 +684,7 @@
 
 
 def sum_kernel(
-    raw, RG, PS, turns, gain, XT, XA, XB, W, WA, WB,
+    raw, RG, PS, turns, gain, XT, XG, W, W2,
     IG, WG,
     xg, w, w2, gg, theirs, acc, acc1, two, acc2, near, acc3, three, wg, send, recv, local,
 ):
@@ -742,11 +707,10 @@
     for steps in (3, 1, 2):
         for kind in range(2):
             c = lax.rem(place[kind] + steps, 4)
-            fetch(steps, XA.at[kind, c], xg.at[0, kind, c])
-            fetch(steps, XB.at[kind, c], xg.at[1, kind, c])
+            for z in range(2):
+                fetch(steps, XG.at[z, kind, c], xg.at[z, kind, c])
     fetch("w", W, w)
-    fetch("w", WA, w2.at[pl.ds(0, 2)])
-    fetch("w", WB, w2.at[pl.ds(2, 2)])
+    fetch("w", W2, w2)
 
     def ready(name):
         for made in fetched[name]:
@@ -938,14 +902,14 @@
     assert links.used <= SUM_COPIES
 
 
-def sum_terms(raw, RG, PS, turns, gain, XT, XA, XB, W, WA, WB):
+def sum_terms(raw, RG, PS, turns, gain, XT, XG, W, W2):
     return pl.pallas_call(
         sum_kernel,
         out_shape=(
             jax.ShapeDtypeStruct((DEV, WIDTH), bf16),
             jax.ShapeDtypeStruct((2, 2, 4, HALF, HEAD), bf16),
         ),
-        in_specs=[VMEM] * 5 + [HBM] * 6,
+        in_specs=[VMEM] * 5 + [HBM] * 4,
         out_specs=(VMEM, VMEM),
         scratch_shapes=[
             pltpu.VMEM((2, 2, 4, 4, ROWS, 2 * DEV), bf16),
@@ -967,7 +931,7 @@
         ],
         compiler_params=remote_params(4),
         name="sum_terms",
-    )(raw, RG, PS, turns, gain, XT, XA, XB, W, WA, WB)
+    )(raw, RG, PS, turns, gain, XT, XG, W, W2)
 
 
 def put_kernel(IG, WG, QG, QO, resp, prompt, qgrad, kout, vout):
@@ -978,7 +942,7 @@
 
     @pl.when(step == core)
     def _():
-        qgrad[0] = QG[0]
+        qgrad[0] = QG[...]
 
     @pl.when(step != core)
     def _():
@@ -1008,7 +972,7 @@
         in_specs=[
             pl.BlockSpec((DEV, half), lambda i: (0, i)),
             VMEM,
-            pl.BlockSpec((1, TOK, 2048), lambda i: (0, 0, 0)),
+            VMEM,
             VMEM,
         ],
         out_specs=(
@@ -1035,12 +999,10 @@
     flat = W.reshape(4, WIDTH, HEAD)
     XT, raw, keys, vals, pkv, turns = project(seg_start, SS, resp_in, prompt_in, XP, flat, cos, sin, gain)
     XT = XT.reshape(4, 4, 2, ROWS, 2 * DEV)
-    everyone, XA, WA = share(pkv, XT, W)
     numbers = (seg_prompt, seg_start, seg_len, SP, SS, SL, owner)
-    QG, RG, PP = attention(numbers, everyone, keys, vals, queries, out_grad, QP, OP)
-    PS, QO, XB, WB = give_back(PP, QG, XT, W)
-    pieces = [a.reshape(-1, 32, ROWS, HEAD) for a in (W, WA, WB)]
-    IG, WG = sum_terms(raw, RG, PS, turns, gain, XT, XA, XB, *pieces)
+    QG, QO, RG, PS, XG, W2 = attend(numbers, pkv, keys, vals, queries, out_grad, QP, OP, XT, W)
+    pieces = [a.reshape(4, 32, ROWS, HEAD) for a in (W, W2)]
+    IG, WG = sum_terms(raw, RG, PS, turns, gain, XT, XG, *pieces)
     resp, prompt, qgrad, kout, vout = put(IG, WG.reshape(2, 2, 2, ROWS, HEAD), QG, QO)
     return qgrad, resp, prompt, kout, vout
 

time: 158 us -> 148 us (0.937)
  Pallas kernels: 157 us -> 147 us
    pallas_call x3 -> x1, Pallas kernels: 54.9 us -> 41.4 us  [attend(): pl.pallas_call(attend_kernel, out_shape=(jax.ShapeDtypeStruct((TOK, 2048)...]
    pallas_call x1, Pallas kernels: 50.8 us -> 55 us  [sum_terms(): pl.pallas_call(sum_kernel, out_shape=(jax.ShapeDtypeStruct((DEV, WIDTH),...]
where the time goes in v2:
time: 148 us
  Pallas kernels  147 us (99%)
    pallas_call x1, Pallas kernels, sum_terms(): pl.pallas_call(sum_kernel, out_shape=(jax.ShapeDtypeStruct((DEV, WIDTH),...  55 us
    pallas_call x1, Pallas kernels, attend(): pl.pallas_call(attend_kernel, out_shape=(jax.ShapeDtypeStruct((TOK, 2048)...  41.4 us
    pallas_call x1, Pallas kernels, gather(): pl.pallas_call(gather_kernel, out_shape=(jax.ShapeDtypeStruct((4, 4, 4, 2...  38 us
    pallas_call x1, Pallas kernels, project(): pl.pallas_call(project_kernel, out_shape=(jax.ShapeDtypeStruct((WIDTH, 2...  9.53 us
    pallas_call x1, Pallas kernels, put(): pl.pallas_call(put_kernel, out_shape=(jax.ShapeDtypeStruct((1, TOK, WIDTH...  3.5 us

profile of v2, /device:TPU:1, one launch (start us, length us, event | category | flops | bytes accessed | tf_op | source)
XLA Modules:
  0.0 148.2 jit_solution(10427486624794121451)
XLA Ops:
  0.6 38.0 %gather.1 = (bf16[4,4,4,2,160,128]{5,4,3,2,1,0:T(8,128)(2,1)}, bf16[192,5120]{1,0:T(8,128)(2,1)}, bf16[128,2048]{1,0:T(8,128)(2,1)}, bf16[128,2048]{1,0:T(8,128)...) custom-call(bf16[160,512]{1,0:T(8,128)(2,1)} %kw.1, bf16[160,512]{1,0:T(8,128)(2,1)} %vw.1, ...), custom_call_target="tpu_custom_call" | custom-call | tf_op jit(solution)/shard_map/gather/pallas_call | solution.py:394
  38.7 9.5 %project.1 = (bf16[5120,384]{1,0:T(8,128)(2,1)}, f32[2,2,192,128]{3,2,1,0:T(8,128)}, bf16[2,2,192,128]{3,2,1,0:T(8,128)(2,1)}, bf16[2,2,192,128]{3,2,1,0:T(8,128...) custom-call(s32[1,2]{1,0:T(1,128)} %ss.5, s32[1,2]{1,0:T(1,128)} %get-tuple-element.31.SS, ...), custom_call_target="tpu_custom_call" | custom-call | tf_op jit(solution)/shard_map/project/pallas_call | solution.py:471
  48.2 41.4 %attend.1 = (bf16[128,2048]{1,0:T(8,128)(2,1)}, bf16[128,2048]{1,0:T(8,128)(2,1)}, bf16[2,2,2,128,128]{4,3,2,1,0:T(8,128)(2,1)}, f32[4,2,64,128]{3,2,1,0:T(8,128...) custom-call(s32[1,2]{1,0:T(1,128)} %sp.3, s32[1,2]{1,0:T(1,128)} %ss.5, s32[1,2]{1,0:T(1,128)} %sl.3, ...), custom_call_target="tpu_custom_call" | custom-call | tf_op jit(solution)/shard_map/attend/pallas_call | solution.py:648
  89.6 55.0 %sum_terms.1 = (bf16[192,5120]{1,0:T(8,128)(2,1)}, bf16[2,2,4,80,128]{4,3,2,1,0:T(8,128)(2,1)}) custom-call(f32[2,2,192,128]{3,2,1,0:T(8,128)} %get-tuple-element.34.raw, bf16[2,2,2,128,128]{4,3,2,1,0:T(8,128)(2,1)} %get-tuple-element.43.RG, f32[4,2,64,128]{3,2,1,0:T(8,128)} %get-tuple-element.44.PS, f32[2,2,192,128]{3,2,1,0:T(8,128)} %get-tuple-element.45.turns, ...), custom_call_target="tpu_custom_call" | custom-call | tf_op jit(solution)/shard_map/sum_terms/pallas_call | solution.py:906
  144.7 3.5 %put.1 = (bf16[1,128,5120]{2,1,0:T(8,128)(2,1)}, bf16[1,64,5120]{2,1,0:T(8,128)(2,1)}, bf16[1,128,4096]{2,1,0:T(8,128)(2,1)}, bf16[160,512]{1,0:T(8,128)(2,1)}, bf16[160,512]{1,0:T(8,128)(2,1)}) custom-call(bf16[192,5120]{1,0:T(8,128)(2,1)} %get-tuple-element.48.IG, bf16[2,2,2,160,128]{4,3,2,1,0:T(8,128)(2,1)} %bitcast.11, ...), custom_call_target="tpu_custom_call" | custom-call | tf_op jit(solution)/shard_map/put/pallas_call | solution.py:962

commit v3 on v2

--- a/solution.py
+++ b/solution.py
@@ -212,15 +212,7 @@
     def from_place(self, steps):
         return lax.rem(self.place + steps, 4)
 
-    def begin(self):
-        mine = self.XG.at[self.me.core, self.place]
-        jobs = (
-            (0, 2, 0, self.relay.at[0], self.plus),
-            (1, 2, 1, self.relay.at[1], self.minus),
-            (2, 1, None, mine, self.plus),
-            (3, 3, None, mine, self.minus),
-        )
-
+    def send(self, jobs):
         def start(kind):
             for n, steps, h, dst, device in jobs:
                 c = self.from_place(steps)
@@ -232,6 +224,13 @@
         pl.when(self.me.core == 1)(lambda: start(1))
         for n, steps, h, dst, device in jobs:
             self.links.sent.append(self.links.copy(self.n[n], dst, dst, device))
+
+    def begin(self):
+        self.send([(0, 2, 0, self.relay.at[0], self.plus), (1, 2, 1, self.relay.at[1], self.minus)])
+
+    def direct(self):
+        mine = self.XG.at[self.me.core, self.place]
+        self.send([(2, 1, None, mine, self.plus), (3, 3, None, mine, self.minus)])
 
     def forward(self):
         core, n = self.me.core, self.n
@@ -531,8 +530,11 @@
     links.start(weights, W, W2, partner)
     parts[...] = jnp.zeros_like(parts)
     out.forward()
-    columns[0].forward()
     out.finish()
+    for half in columns:
+        half.forward()
+    for half in columns:
+        half.direct()
     for made in locals_:
         made.wait()
 
@@ -615,9 +617,6 @@
 
     lax.fori_loop(2, 4, attend, 0)
     links.start(swapped, made_q.at[1], QO, partner)
-    columns[1].forward()
-    for steps in (3, 1, 2):
-        columns[0].hand_over(steps)
     lax.fori_loop(0, 2, attend, 0)
     PP[...] = parts[...].astype(bf16)
 
@@ -631,10 +630,11 @@
 
     home = Reduce4(links, ring, lambda c, h: PP.at[c, pl.ds(2 * h, 2)], lambda i: land.at[i], add)
     home.begin()
-    for steps in (3, 1, 2):
-        columns[1].hand_over(steps)
     QG[...] = made_q[0]
+    columns[0].hand_over(2)
     home.mid()
+    for half, steps in ((1, 2), (0, 3), (0, 1), (1, 3), (1, 1)):
+        columns[half].hand_over(steps)
     home.finish(lambda h: PS.at[pl.ds(2 * h, 2)])
     columns[0].finish()
     columns[1].finish()
@@ -684,14 +684,13 @@
 
 
 def sum_kernel(
-    raw, RG, PS, turns, gain, XT, XG, W, W2,
+    raw_, RG_, PS_, turns_, gain, XT, XG, W, W2,
     IG, WG,
-    xg, w, w2, gg, theirs, acc, acc1, two, acc2, near, acc3, three, wg, send, recv, local,
+    xg, w, w2, gg, theirs, acc, acc1, two, blocks, near, wg, raw, RG, PS, turns, send, recv, local,
 ):
     me = Place()
     partner = me.partner()
-    near_minus, near_plus = me.near_z()
-    ring_x, ring_y, ring_zh = me.ring_x(), me.ring_y(), me.ring_zh()
+    ring_x, ring_y = me.ring_x(), me.ring_y()
     core, zl = me.core, me.zl
     place = (me.x, me.y)
     fetched = {}
@@ -701,6 +700,8 @@
         made.start()
         fetched.setdefault(name, []).append(made)
 
+    for src, dst in ((raw_, raw), (RG_, RG), (PS_, PS), (turns_, turns)):
+        fetch("small", src, dst)
     for z in range(2):
         fetch(0, XT.at[:, me.x, z], xg.at[z, 0, me.x])
         fetch(0, XT.at[me.y, :, z], xg.at[z, 1, me.y])
@@ -716,7 +717,8 @@
         for made in fetched[name]:
             made.wait()
 
-    greet([*ring_x[1:], *ring_y[1:], *ring_zh[1:], near_minus, near_plus, partner])
+    greet([*ring_x[1:], *ring_y[1:], *[me.at(z=lax.rem(me.z + k, 8)) for k in range(1, 8)], partner])
+    ready("small")
     links = Links(send, recv)
 
     for d in range(2):
@@ -804,32 +806,33 @@
 
     class Wave:
         def __init__(self, n):
-            self.n, self.slots = n, (n, 2 + n)
-            self.pair = [(links.take(), near_plus), (links.take(), near_minus)]
-            self.third = Reduce4(
-                links, ring_zh, lambda c, h: acc3.at[n, c, cut[h]], lambda i: three.at[n, i, thirds[i]], add_block
+            self.n = n
+            self.down = [links.take() for _ in range(7)]
+            self.round = [links.take() for _ in range(3)]
+            self.across = links.take()
+
+        def sum_begin(self):
+            for k in (4, 3, 5, 2, 6, 1, 7):
+                z = lax.rem(me.z + k, 8)
+                block = blocks.at[self.n, lax.rem(z, 2), lax.div(z, 2)]
+                links.start(self.down[k - 1], block, near.at[self.n, k - 1], me.at(z=z))
+
+        def sum_finish(self):
+            for k in range(1, 8):
+                links.arrived(self.down[k - 1], near.at[self.n, k - 1], partner)
+            add_block(
+                wg.at[core, self.n, me.zh],
+                [blocks.at[self.n, zl, me.zh]] + [near.at[self.n, k] for k in range(7)],
             )
-            self.last = Gather4(
-                links, ring_zh, lambda c: wg.at[core, n, c], lambda c, h: wg.at[core, n, c, cut[h]]
-            )
-            self.across = links.take()
-
-        def near_begin(self):
-            for kind, (number, device) in enumerate(self.pair):
-                links.start(number, acc2.at[self.slots[kind], 1 - zl], near.at[self.n, kind], device)
-
-        def near_finish(self):
-            for kind, (number, device) in enumerate(self.pair):
-                links.arrived(number, near.at[self.n, kind], device)
-                for h in range(2):
-                    rows = pl.ds(h * HALF, HALF)
-                    add_block(
-                        acc3.at[self.n, 2 * kind + h],
-                        [acc2.at[self.slots[kind], zl, rows], near.at[self.n, kind, rows]],
-                    )
-
-        def third_finish(self):
-            self.third.finish(lambda h: wg.at[core, self.n, me.zh, cut[h]])
+
+        def round_begin(self):
+            mine = wg.at[core, self.n, me.zh]
+            for k in (2, 1, 3):
+                links.start(self.round[k - 1], mine, mine, me.at(z=lax.rem(me.z + 2 * k, 8)))
+
+        def round_finish(self):
+            for k in (1, 2, 3):
+                links.arrived(self.round[k - 1], wg.at[core, self.n, lax.rem(me.zh + 4 - k, 4)], partner)
 
         def across_begin(self):
             links.start(self.across, wg.at[core, self.n], wg.at[core, self.n], partner)
@@ -837,8 +840,6 @@
         def across_finish(self):
             links.arrived(self.across, wg.at[1 - core, self.n], partner)
 
-    cut = (pl.ds(0, 48), pl.ds(48, 32))
-    thirds = [cut[h] for h in (0, 1, 1, 0, 0, 1)]
     waves = Wave(0), Wave(1)
 
     ready(0)
@@ -860,7 +861,16 @@
         links.arrived(crossed[kind], theirs.at[kind], partner)
 
     def settle(t):
-        second[t].finish(lambda h: acc2.at[t, h])
+        def add(dst, terms):
+            total = terms[0][...].astype(f32)
+            for term in terms[1:]:
+                total = total + term[...].astype(f32)
+            total = total.astype(bf16)
+            for i in range(2):
+                dst[2 * (t // 2) + i] = total[i * HALF : (i + 1) * HALF]
+
+        second[t].add = add
+        second[t].finish(lambda h: blocks.at[t % 2, h])
 
     input_parts(0, 1)
     second[0].mid()
@@ -870,31 +880,21 @@
     input_parts(1, 2)
     settle(0)
     settle(2)
-    waves[0].near_begin()
-    input_parts(2, 3)
-    waves[0].near_finish()
-    waves[0].third.begin()
+    waves[0].sum_begin()
     settle(1)
     settle(3)
-    waves[1].near_begin()
-    waves[0].third.mid()
-    waves[1].near_finish()
-    waves[1].third.begin()
-    input_parts(3, 4)
-    waves[0].third_finish()
-    waves[0].last.begin()
-    waves[1].third.mid()
-    input_parts(4, 5)
-    waves[0].last.forward()
-    waves[1].third_finish()
-    waves[1].last.begin()
-    input_parts(5, 7)
-    waves[0].last.finish()
+    waves[1].sum_begin()
+    input_parts(2, 4)
+    waves[0].sum_finish()
+    waves[0].round_begin()
+    waves[1].sum_finish()
+    waves[1].round_begin()
+    input_parts(4, 6)
+    waves[0].round_finish()
     waves[0].across_begin()
-    waves[1].last.forward()
-    input_parts(7, 8)
-    waves[1].last.finish()
+    waves[1].round_finish()
     waves[1].across_begin()
+    input_parts(6, 8)
     waves[0].across_finish()
     waves[1].across_finish()
     WG[...] = wg[...]
@@ -909,7 +909,7 @@
             jax.ShapeDtypeStruct((DEV, WIDTH), bf16),
             jax.ShapeDtypeStruct((2, 2, 4, HALF, HEAD), bf16),
         ),
-        in_specs=[VMEM] * 5 + [HBM] * 4,
+        in_specs=[HBM] * 4 + [VMEM] + [HBM] * 4,
         out_specs=(VMEM, VMEM),
         scratch_shapes=[
             pltpu.VMEM((2, 2, 4, 4, ROWS, 2 * DEV), bf16),
@@ -920,14 +920,16 @@
             pltpu.VMEM((2, 2, 4 * ROWS, 256), f32),
             pltpu.VMEM((4, 4, 2, ROWS, HEAD), bf16),
             pltpu.VMEM((4, 6, ROWS, HEAD), bf16),
-            pltpu.VMEM((4, 2, ROWS, HEAD), bf16),
-            pltpu.VMEM((2, 2, ROWS, HEAD), bf16),
-            pltpu.VMEM((2, 4, HALF, HEAD), bf16),
-            pltpu.VMEM((2, 6, HALF, HEAD), bf16),
             pltpu.VMEM((2, 2, 4, HALF, HEAD), bf16),
+            pltpu.VMEM((2, 7, HALF, HEAD), bf16),
+            pltpu.VMEM((2, 2, 4, HALF, HEAD), bf16),
+            pltpu.VMEM((2, 2, DEV, HEAD), f32),
+            pltpu.VMEM((2, 2, 2, TOK, HEAD), bf16),
+            pltpu.VMEM((4, 2, PRO, HEAD), f32),
+            pltpu.VMEM((2, 2, DEV, HEAD), f32),
             pltpu.SemaphoreType.DMA((SUM_COPIES,)),
             pltpu.SemaphoreType.DMA((SUM_COPIES,)),
-            pltpu.SemaphoreType.DMA((20,)),
+            pltpu.SemaphoreType.DMA((24,)),
         ],
         compiler_params=remote_params(4),
         name="sum_terms",

time: 148 us -> 137 us (0.926)
  Pallas kernels: 147 us -> 136 us
    pallas_call x1, Pallas kernels: 55 us -> 43.9 us  [sum_terms(): pl.pallas_call(sum_kernel, out_shape=(jax.ShapeDtypeStruct((DEV, WIDTH),...]
where the time goes in v3:
time: 137 us
  Pallas kernels  136 us (99%)
    pallas_call x1, Pallas kernels, sum_terms(): pl.pallas_call(sum_kernel, out_shape=(jax.ShapeDtypeStruct((DEV, WIDTH),...  43.9 us
    pallas_call x1, Pallas kernels, attend(): pl.pallas_call(attend_kernel, out_shape=(jax.ShapeDtypeStruct((TOK, 2048)...  41.1 us
    pallas_call x1, Pallas kernels, gather(): pl.pallas_call(gather_kernel, out_shape=(jax.ShapeDtypeStruct((4, 4, 4, 2...  38 us
    pallas_call x1, Pallas kernels, project(): pl.pallas_call(project_kernel, out_shape=(jax.ShapeDtypeStruct((WIDTH, 2...  9.53 us
    pallas_call x1, Pallas kernels, put(): pl.pallas_call(put_kernel, out_shape=(jax.ShapeDtypeStruct((1, TOK, WIDTH...  3.5 us

profile of v3, /device:TPU:1, one launch (start us, length us, event | category | flops | bytes accessed | tf_op | source)
XLA Modules:
  0.0 136.7 jit_solution(8371325685160296574)
XLA Ops:
  0.6 38.0 %gather.1 = (bf16[4,4,4,2,160,128]{5,4,3,2,1,0:T(8,128)(2,1)}, bf16[192,5120]{1,0:T(8,128)(2,1)}, bf16[128,2048]{1,0:T(8,128)(2,1)}, bf16[128,2048]{1,0:T(8,128)...) custom-call(bf16[160,512]{1,0:T(8,128)(2,1)} %kw.1, bf16[160,512]{1,0:T(8,128)(2,1)} %vw.1, ...), custom_call_target="tpu_custom_call" | custom-call | tf_op jit(solution)/shard_map/gather/pallas_call | solution.py:393
  38.7 9.5 %project.1 = (bf16[5120,384]{1,0:T(8,128)(2,1)}, f32[2,2,192,128]{3,2,1,0:T(8,128)}, bf16[2,2,192,128]{3,2,1,0:T(8,128)(2,1)}, bf16[2,2,192,128]{3,2,1,0:T(8,128...) custom-call(s32[1,2]{1,0:T(1,128)} %ss.5, s32[1,2]{1,0:T(1,128)} %get-tuple-element.31.SS, ...), custom_call_target="tpu_custom_call" | custom-call | tf_op jit(solution)/shard_map/project/pallas_call | solution.py:470
  48.2 41.1 %attend.1 = (bf16[128,2048]{1,0:T(8,128)(2,1)}, bf16[128,2048]{1,0:T(8,128)(2,1)}, bf16[2,2,2,128,128]{4,3,2,1,0:T(8,128)(2,1)}, f32[4,2,64,128]{3,2,1,0:T(8,128...) custom-call(s32[1,2]{1,0:T(1,128)} %sp.3, s32[1,2]{1,0:T(1,128)} %ss.5, s32[1,2]{1,0:T(1,128)} %sl.3, ...), custom_call_target="tpu_custom_call" | custom-call | tf_op jit(solution)/shard_map/attend/pallas_call | solution.py:648
  89.3 43.9 %sum_terms.1 = (bf16[192,5120]{1,0:T(8,128)(2,1)}, bf16[2,2,4,80,128]{4,3,2,1,0:T(8,128)(2,1)}) custom-call(f32[2,2,192,128]{3,2,1,0:T(8,128)} %get-tuple-element.34.raw_, bf16[2,2,2,128,128]{4,3,2,1,0:T(8,128)(2,1)} %get-tuple-element.43.RG_, f32[4,2,64,128]{3,2,1,0:T(8,128)} %get-tuple-element.44.PS_, f32[2,2,192,128]{3,2,1,0:T(8,128)} %get-tuple-element.45.turns_, ...), custom_call_target="tpu_custom_call" | custom-call | tf_op jit(solution)/shard_map/sum_terms/pallas_call | solution.py:906
  133.2 3.5 %put.1 = (bf16[1,128,5120]{2,1,0:T(8,128)(2,1)}, bf16[1,64,5120]{2,1,0:T(8,128)(2,1)}, bf16[1,128,4096]{2,1,0:T(8,128)(2,1)}, bf16[160,512]{1,0:T(8,128)(2,1)}, bf16[160,512]{1,0:T(8,128)(2,1)}) custom-call(bf16[192,5120]{1,0:T(8,128)(2,1)} %get-tuple-element.48.IG, bf16[2,2,2,160,128]{4,3,2,1,0:T(8,128)(2,1)} %bitcast.11, ...), custom_call_target="tpu_custom_call" | custom-call | tf_op jit(solution)/shard_map/put/pallas_call | solution.py:964

commit v4 on v3

--- a/solution.py
+++ b/solution.py
@@ -846,6 +846,10 @@
     terms_of(0)
     for going in rounds:
         going.forward()
+    ready("w")
+    for kind in range(2):
+        links.arrived(crossed[kind], theirs.at[kind], partner)
+    input_parts(0, 2)
     ready(3)
     terms_of(3)
     ready(1)
@@ -856,9 +860,6 @@
     terms_of(2)
     for t in (0, 2, 1, 3):
         second[t].begin()
-    ready("w")
-    for kind in range(2):
-        links.arrived(crossed[kind], theirs.at[kind], partner)
 
     def settle(t):
         def add(dst, terms):
@@ -872,29 +873,28 @@
         second[t].add = add
         second[t].finish(lambda h: blocks.at[t % 2, h])
 
-    input_parts(0, 1)
+    input_parts(2, 3)
     second[0].mid()
     second[2].mid()
     second[1].mid()
     second[3].mid()
-    input_parts(1, 2)
+    input_parts(3, 4)
     settle(0)
     settle(2)
     waves[0].sum_begin()
     settle(1)
     settle(3)
     waves[1].sum_begin()
-    input_parts(2, 4)
+    input_parts(4, 6)
     waves[0].sum_finish()
     waves[0].round_begin()
     waves[1].sum_finish()
     waves[1].round_begin()
-    input_parts(4, 6)
+    input_parts(6, 8)
     waves[0].round_finish()
     waves[0].across_begin()
     waves[1].round_finish()
     waves[1].across_begin()
-    input_parts(6, 8)
     waves[0].across_finish()
     waves[1].across_finish()
     WG[...] = wg[...]
@@ -942,11 +942,11 @@
     resp[0] = IG[:TOK]
     prompt[0] = IG[TOK:]
 
-    @pl.when(step == core)
+    @pl.when(step // 2 == core)
     def _():
         qgrad[0] = QG[...]
 
-    @pl.when(step != core)
+    @pl.when(step // 2 != core)
     def _():
         qgrad[0] = QO[...]
 
@@ -960,7 +960,7 @@
 
 
 def put(IG, WG, QG, QO):
-    half = WIDTH // 2
+    part = WIDTH // 4
     return pl.pallas_call(
         put_kernel,
         out_shape=(
@@ -970,17 +970,17 @@
             jax.ShapeDtypeStruct((ROWS, 512), bf16),
             jax.ShapeDtypeStruct((ROWS, 512), bf16),
         ),
-        grid=(2,),
+        grid=(4,),
         in_specs=[
-            pl.BlockSpec((DEV, half), lambda i: (0, i)),
+            pl.BlockSpec((DEV, part), lambda i: (0, i)),
             VMEM,
-            VMEM,
-            VMEM,
+            pl.BlockSpec((TOK, 1024), lambda i: (0, lax.rem(i, 2))),
+            pl.BlockSpec((TOK, 1024), lambda i: (0, lax.rem(i, 2))),
         ],
         out_specs=(
-            pl.BlockSpec((1, TOK, half), lambda i: (0, 0, i)),
-            pl.BlockSpec((1, PRO, half), lambda i: (0, 0, i)),
-            pl.BlockSpec((1, TOK, 2048), lambda i: (0, 0, i)),
+            pl.BlockSpec((1, TOK, part), lambda i: (0, 0, i)),
+            pl.BlockSpec((1, PRO, part), lambda i: (0, 0, i)),
+            pl.BlockSpec((1, TOK, 1024), lambda i: (0, 0, i)),
             VMEM,
             VMEM,
         ),

time: 137 us -> 138 us (level)
  no operation moved by 1% of the time
where the time goes in v4:
time: 138 us
  Pallas kernels  137 us (99%)
    pallas_call x1, Pallas kernels, sum_terms(): pl.pallas_call(sum_kernel, out_shape=(jax.ShapeDtypeStruct((DEV, WIDTH),...  44 us
    pallas_call x1, Pallas kernels, attend(): pl.pallas_call(attend_kernel, out_shape=(jax.ShapeDtypeStruct((TOK, 2048)...  41.1 us
    pallas_call x1, Pallas kernels, gather(): pl.pallas_call(gather_kernel, out_shape=(jax.ShapeDtypeStruct((4, 4, 4, 2...  38 us
    pallas_call x1, Pallas kernels, project(): pl.pallas_call(project_kernel, out_shape=(jax.ShapeDtypeStruct((WIDTH, 2...  9.53 us
    pallas_call x1, Pallas kernels, put(): pl.pallas_call(put_kernel, out_shape=(jax.ShapeDtypeStruct((1, TOK, WIDTH...  4.65 us

profile of v4, /device:TPU:1, one launch (start us, length us, event | category | flops | bytes accessed | tf_op | source)
XLA Modules:
  0.0 138.0 jit_solution(4740218730355408529)
XLA Ops:
  0.6 38.0 %gather.1 = (bf16[4,4,4,2,160,128]{5,4,3,2,1,0:T(8,128)(2,1)}, bf16[192,5120]{1,0:T(8,128)(2,1)}, bf16[128,2048]{1,0:T(8,128)(2,1)}, bf16[128,2048]{1,0:T(8,128)...) custom-call(bf16[160,512]{1,0:T(8,128)(2,1)} %kw.1, bf16[160,512]{1,0:T(8,128)(2,1)} %vw.1, ...), custom_call_target="tpu_custom_call" | custom-call | tf_op jit(solution)/shard_map/gather/pallas_call | solution.py:393
  38.7 9.5 %project.1 = (bf16[5120,384]{1,0:T(8,128)(2,1)}, f32[2,2,192,128]{3,2,1,0:T(8,128)}, bf16[2,2,192,128]{3,2,1,0:T(8,128)(2,1)}, bf16[2,2,192,128]{3,2,1,0:T(8,128...) custom-call(s32[1,2]{1,0:T(1,128)} %ss.5, s32[1,2]{1,0:T(1,128)} %get-tuple-element.31.SS, ...), custom_call_target="tpu_custom_call" | custom-call | tf_op jit(solution)/shard_map/project/pallas_call | solution.py:470
  48.2 41.1 %attend.1 = (bf16[128,2048]{1,0:T(8,128)(2,1)}, bf16[128,2048]{1,0:T(8,128)(2,1)}, bf16[2,2,2,128,128]{4,3,2,1,0:T(8,128)(2,1)}, f32[4,2,64,128]{3,2,1,0:T(8,128...) custom-call(s32[1,2]{1,0:T(1,128)} %sp.3, s32[1,2]{1,0:T(1,128)} %ss.5, s32[1,2]{1,0:T(1,128)} %sl.3, ...), custom_call_target="tpu_custom_call" | custom-call | tf_op jit(solution)/shard_map/attend/pallas_call | solution.py:648
  89.3 44.0 %sum_terms.1 = (bf16[192,5120]{1,0:T(8,128)(2,1)}, bf16[2,2,4,80,128]{4,3,2,1,0:T(8,128)(2,1)}) custom-call(f32[2,2,192,128]{3,2,1,0:T(8,128)} %get-tuple-element.34.raw_, bf16[2,2,2,128,128]{4,3,2,1,0:T(8,128)(2,1)} %get-tuple-element.43.RG_, f32[4,2,64,128]{3,2,1,0:T(8,128)} %get-tuple-element.44.PS_, f32[2,2,192,128]{3,2,1,0:T(8,128)} %get-tuple-element.45.turns_, ...), custom_call_target="tpu_custom_call" | custom-call | tf_op jit(solution)/shard_map/sum_terms/pallas_call | solution.py:906
  133.3 4.7 %put.1 = (bf16[1,128,5120]{2,1,0:T(8,128)(2,1)}, bf16[1,64,5120]{2,1,0:T(8,128)(2,1)}, bf16[1,128,4096]{2,1,0:T(8,128)(2,1)}, bf16[160,512]{1,0:T(8,128)(2,1)}, bf16[160,512]{1,0:T(8,128)(2,1)}) custom-call(bf16[192,5120]{1,0:T(8,128)(2,1)} %get-tuple-element.48.IG, bf16[2,2,2,160,128]{4,3,2,1,0:T(8,128)(2,1)} %bitcast.11, ...), custom_call_target="tpu_custom_call" | custom-call | tf_op jit(solution)/shard_map/put/pallas_call | solution.py:964
